TPU v7x, 256 devices: a whole 4x4x8 slice. The times are simulated.
256 devices in a mesh: band: 8 (over x_lo, y), dom: 32 (over x_hi, z, core).
Axes of the slice: x: 4 (x_hi: 2, x_lo: 2; x = x_hi * 2 + x_lo), y: 4, z: 8, core: 2. Of those that a mesh axis runs over, the one named last changes fastest.
Arguments:
- partial_density: float32 [8, 192, 96, 128], P('band', 'dom'), may hold values from 0.002 to 0.1
- moments: bfloat16 [9, 256], P(None, 'dom'), may hold values from 0.0099487305 to 0.099609375
- shape_functions: bfloat16 [256, 9, 6912], P('dom'), may hold values from 0.099609375 to 1
- sphere_offsets: int32 [3, 256], P(None, 'dom'), may hold values from 0 to 232, as said below
- owned_count: int32 [32], P('dom'), may hold values from 1 to 8, as said below
Outputs:
- potential: float32 [192, 96, 128], P('dom')
Inputs may be any that keep to these rules, and one draw needn't show every extreme that they name: `sphere_offsets`: row 0 lies in 0 to 11, and in 0 to 0 for the last slab; row 1 in 0 to 168; row 2 in 0 to 232; each upper end is reached. `owned_count`: some slab owns exactly 8 atoms.
All inputs are finite; a program needn't handle non-finite values.
Results may differ from a plain program's by a relative error of at most 0.0003.
Values sent between devices are 32-bit elements; how exact they have to be, the bound alone decides.
No kernel may reach another device: no remote copies, remote signals or barrier semaphores. Data moves between devices by JAX's collectives and lax.ppermute only.
A program may use at most 64 MiB of HBM per device.

v0:
```python
import jax
import jax.numpy as jnp
from jax import lax
from jax.sharding import PartitionSpec as P

SBX = 12
SBY = 24
SBZ = 24


kappa_pbe = 0.804
mu_pbe = 0.2195
exchange_prefactor = -0.75 * (3.0 / 3.141592653589793) ** (1.0 / 3.0)
gradient_scale = 4.0 * (3.0 * 3.141592653589793**2) ** (2.0 / 3.0)
half_inverse = 0.5 / 0.2


def from_behind(block, axis, distance):
    devices = range(lax.axis_size(axis))
    route = [(i - distance, i) for i in devices if i - distance in devices]
    return lax.ppermute(block, axis, route)


def extended_2(cells, sides, width):
    for axis, dim in sides:
        count = lax.axis_size(axis)
        ends = count - 1
        head = lax.slice_in_dim(cells, 0, width, axis=dim)
        tail = lax.slice_in_dim(cells, cells.shape[dim] - width, cells.shape[dim], axis=dim)
        cells = jnp.concatenate(
            [
                lax.ppermute(tail, axis, [(i, (i + 1) % count) for i in range(ends)]),
                cells,
                lax.ppermute(head, axis, [((i + 1) % count, i) for i in range(ends)]),
            ],
            axis=dim,
        )
    return cells


def refine(extended, direction):
    length = extended.shape[direction] - 2
    lower_cells = lax.slice_in_dim(extended, 0, length, axis=direction)
    middle_cells = lax.slice_in_dim(extended, 1, length + 1, axis=direction)
    upper_cells = lax.slice_in_dim(extended, 2, length + 2, axis=direction)
    even_cells = 0.75 * middle_cells + 0.25 * lower_cells
    odd_cells = 0.75 * middle_cells + 0.25 * upper_cells
    joined = jnp.stack([even_cells, odd_cells], axis=direction + 1)
    target = list(middle_cells.shape)
    target[direction] = 2 * length
    return joined.reshape(target)


def restrict(extended, direction):
    doubled = extended.shape[direction] - 2
    halved = doubled // 2

    def paired(start):
        piece = lax.slice_in_dim(extended, start, start + doubled, axis=direction)
        target = list(piece.shape)
        target[direction : direction + 1] = [halved, 2]
        return piece.reshape(target)

    centre = paired(1)
    outer_low = lax.index_in_dim(paired(0), 0, direction + 1, keepdims=False)
    outer_high = lax.index_in_dim(paired(2), 1, direction + 1, keepdims=False)
    first_half = lax.index_in_dim(centre, 0, direction + 1, keepdims=False)
    second_half = lax.index_in_dim(centre, 1, direction + 1, keepdims=False)
    return 0.125 * outer_low + 0.375 * (first_half + second_half) + 0.125 * outer_high


def exchange_parts(density, sigma):
    cube_root = jnp.cbrt(density)
    four_thirds = density * cube_root
    reduced = sigma / (gradient_scale * four_thirds * four_thirds)
    damped = 1.0 + mu_pbe * reduced / kappa_pbe
    enhance = 1.0 + kappa_pbe - kappa_pbe / damped
    slope = mu_pbe / (damped * damped)
    by_density = (
        exchange_prefactor * cube_root * (4.0 / 3.0 * enhance - 8.0 / 3.0 * reduced * slope)
    )
    by_sigma = exchange_prefactor * slope / (gradient_scale * four_thirds)
    return (by_density, by_sigma)


def selector(offset, extent, length):
    inside = jnp.arange(extent)
    target = jnp.arange(length)
    return (offset[:, None, None] + inside[None, :, None] == target[None, None, :]).astype(
        jnp.float32
    )


def place(blocks, row_offset, col_offset, depth_offset, rows_out, cols_out, depth_out):
    slot_count = blocks.shape[0]
    cube = blocks.reshape(slot_count, SBX, SBY, SBZ)
    pick_rows = selector(row_offset, SBX, rows_out)
    pick_cols = selector(col_offset, SBY, cols_out)
    pick_depth = selector(depth_offset, SBZ, depth_out)
    highest = lax.Precision.HIGHEST
    section_rows = jnp.einsum("sabc,sax->sxbc", cube, pick_rows, precision=highest)
    section_cols = jnp.einsum("sxbc,sby->sxcy", section_rows, pick_cols, precision=highest)
    return jnp.einsum("sxcy,scz->xyz", section_cols, pick_depth, precision=highest)


def transform(coarse, spheres, coarse_rim, face_rim, fine_rim):
    fine = coarse_rim(coarse)
    for direction in range(3):
        fine = refine(fine, direction)
    density = fine + spheres
    extended = face_rim(density[None])[0]
    grad_x = (extended[2:, 1:-1, 1:-1] - extended[:-2, 1:-1, 1:-1]) * half_inverse
    grad_y = (extended[1:-1, 2:, 1:-1] - extended[1:-1, :-2, 1:-1]) * half_inverse
    grad_z = (extended[1:-1, 1:-1, 2:] - extended[1:-1, 1:-1, :-2]) * half_inverse
    sigma = grad_x * grad_x + grad_y * grad_y + grad_z * grad_z
    by_density, by_sigma = exchange_parts(density, sigma)
    flux = jnp.stack([2.0 * by_sigma * grad_x, 2.0 * by_sigma * grad_y, 2.0 * by_sigma * grad_z])
    flux_ext = face_rim(flux)
    spread = flux_ext[0, 2:, 1:-1, 1:-1] - flux_ext[0, :-2, 1:-1, 1:-1]
    spread = spread + flux_ext[1, 1:-1, 2:, 1:-1] - flux_ext[1, 1:-1, :-2, 1:-1]
    spread = spread + flux_ext[2, 1:-1, 1:-1, 2:] - flux_ext[2, 1:-1, 1:-1, :-2]
    fine_potential = by_density - spread * half_inverse
    result = fine_rim(fine_potential)
    for direction in range(3):
        result = restrict(result, direction)
    return result


def body(partial_density, moments, shape_functions, sphere_offsets, owned_count):
    coarse_x = partial_density.shape[1]
    coarse_y = partial_density.shape[2]
    fine_x = 2 * coarse_x
    fine_y = 2 * coarse_y
    fine_z = 2 * partial_density.shape[3]
    slot_total = moments.shape[1]
    live = (jnp.arange(slot_total) < owned_count[0]).astype(jnp.bfloat16)
    blocks = jnp.einsum(
        "ls,slk->sk", moments * live[None, :], shape_functions, preferred_element_type=jnp.float32
    )
    buffer = place(
        blocks,
        sphere_offsets[0],
        sphere_offsets[1],
        sphere_offsets[2],
        fine_x + SBX,
        fine_y,
        fine_z,
    )
    own_spheres = buffer[:fine_x]
    arrived = from_behind(buffer[fine_x:], "dom", 1)
    own_spheres = own_spheres.at[:SBX].add(arrived)
    coarse = lax.psum(partial_density, "band")[0]

    def coarse_rim(field):
        padded = extended_2(field, (("dom", 0),), 1)
        return jnp.pad(padded, ((0, 0), (1, 1), (1, 1)))

    def face_rim(field):
        padded = extended_2(field, (("dom", 1),), 1)
        return jnp.pad(padded, ((0, 0), (0, 0), (1, 1), (1, 1)))

    def fine_rim(field):
        padded = extended_2(field, (("dom", 0),), 1)
        return jnp.pad(padded, ((0, 0), (1, 1), (1, 1)))

    return transform(coarse, own_spheres, coarse_rim, face_rim, fine_rim)


def solution(mesh):
    return jax.shard_map(
        body,
        mesh=mesh,
        in_specs=(
            P("band", "dom", None, None),
            P(None, "dom"),
            P("dom", None, None),
            P(None, "dom"),
            P("dom"),
        ),
        out_specs=P("dom", None, None),
        check_vma=False,
    )
```

profile of v0, /device:TPU:4, one launch (start us, length us, event | category | flops | bytes accessed | tf_op | source)
XLA Modules:
  0.0 254.0 jit_solution(7494920957338681490)
XLA Ops:
  11.7 2.2 fusion.21
  13.9 4.7 %convolution_bitcast_fusion = f32[24,192,256]{2,1,0:T(8,128)S(1)} fusion(f32[8,24,24,192]{3,2,0,1:T(8,128)S(1)} %fusion.21, s32[8,24]{1,0:T(8,128)S(1)} %get-tuple-element.55), kind=kOutput, calls=%fused_computation.67 | convolution fusion | flops 2717958144 | bytes 8258304 | tf_op jit(solution)/shard_map/sxcy,scz->xyz/dot_general | solution.py:103
  21.5 1.9 collective-permute-start.2
  24.4 91.4 %all-reduce.6.cloned.1.call-done = f32[1,6,96,128]{2,3,1,0:T(8,128)} async-done(((f32[1,6,96,128]{2,3,1,0:T(8,128)}), f32[1,6,96,128]{2,3,1,0:T(8,128)}) %all-reduce.6.cloned.1.call-update) | async-done | bytes 294928 | tf_op jit(solution)/shard_map/psum | solution.py:152
  116.7 1.9 collective-permute-start
  118.6 7.4 %collective-permute-start.1 = (f32[1,96,128]{1,2,0:T(8,128)S(1)}, f32[1,96,128]{1,2,0:T(8,128)S(1)}, u32[]{:S(2)}, u32[]{:S(2)}) collective-permute-start(f32[1,96,128]{1,2,0:T(8,128)S(1)} %get-tuple-element.51), channel_id=1, source_target_pairs={{1,0},{2,1},{3,2},{4,3},{5,4},{6,5},{7,6},{8,7},{9,8},{10,9},{11,1... | collective-permute-start | bytes 147464 | tf_op jit(solution)/shard_map/ppermute | solution.py:34
  129.8 2.6 %copy.11 = f32[12,96,2,130]{3,2,1,0:T(2,128)} copy(f32[12,96,2,130]{1,3,0,2:T(8,128)S(1)} %pad_maximum_fusion.7) | data formatting | bytes 2396160 | tf_op jit(solution)/shard_map/stack | solution.py:48
  132.3 3.1 %reshape.194 = f32[12,192,130]{2,1,0:T(8,128)S(1)} reshape(f32[12,96,2,130]{3,2,1,0:T(2,128)} %copy.11) | data formatting | bytes 2396160 | tf_op jit(solution)/shard_map/reshape | solution.py:51
  137.7 4.0 %copy.12 = f32[12,192,128,2]{1,3,2,0:T(2,128)S(1)} copy(f32[12,192,128,2]{2,1,0,3:T(8,128)} %pad_maximum_fusion.6) | data formatting | bytes 4718592 | tf_op jit(solution)/shard_map/stack | solution.py:48
  141.8 3.4 %reshape.195 = f32[12,192,256]{1,2,0:T(8,128)} reshape(f32[12,192,128,2]{1,3,2,0:T(2,128)S(1)} %copy.12) | data formatting | bytes 4718592 | tf_op jit(solution)/shard_map/reshape | solution.py:51
  145.2 2.3 copy.13
  147.6 2.8 %fusion.20 = f32[12,192,256]{2,1,0:T(8,128)S(1)} fusion(f32[12,192,256]{2,1,0:T(8,128)S(1)} %copy.13, f32[12,192,256]{2,1,0:T(8,128)} %collective-permute-done.2, f32[24,192,256]{2,1,0:T(8,128)} %copy-done.3), kind=kLoop, calls=%fused_computation.58 | loop fusion | flops 1179648 | bytes 9437184 | tf_op jit(solution)/shard_map/add | solution.py:110
  150.4 1.9 collective-permute-start.3
  152.4 7.3 %collective-permute-start.4 = (f32[1,1,192,256]{3,2,1,0:T(8,128)S(1)}, f32[1,1,192,256]{3,2,1,0:T(8,128)S(1)}, u32[]{:S(2)}, u32[]{:S(2)}) collective-permute-start(f32[1,1,192,256]{3,2,1,0:T(8,128)S(1)} %get-tuple-element.37), channel_id=1, source_target_pairs={{1,0},{2,1},{3,2},{4,3},{5,4},{6,5},{7,6},{8,7},{9,8},{10,9},{11,1... | collective-permute-start | bytes 589832 | tf_op jit(solution)/shard_map/ppermute | solution.py:34
  161.1 1.8 collective-permute-done.4
  162.8 2.6 %fusion.3 = f32[14,194,258]{2,1,0:T(8,128)S(1)} fusion(f32[1,1,192,256]{3,2,1,0:T(8,128)S(1)} %collective-permute-done.4, f32[1,12,192,256]{3,2,1,0:T(8,128)S(1)} %bitcast.104, f32[1,1,192,256]{3,2,1,0:T(8,128)S(1)} %collective-permute-done.3), kind=kLoop, calls=%fused_computation.22 | loop fusion | flops 10510920 | bytes 5555424 | tf_op jit(solution)/shard_map/squeeze | solution.py:111
  165.4 6.0 %multiply_bitcast_fusion.2 = (f32[1,12,192,256]{3,2,1,0:T(8,128)S(1)}, f32[12,192,256]{2,1,0:T(8,128)S(1)}) fusion(f32[14,194,258]{2,1,0:T(8,128)S(1)} %fusion.3, f32[12,192,256]{2,1,0:T(8,128)S(1)} %fusion.20), kind=kLoop, calls=%fused_computation.64 | loop fusion | flops 13565952 | bytes 21233664 | tf_op jit(solution)/shard_map/stack | solution.py:117
  171.5 4.4 %multiply_bitcast_fusion.1 = (f32[1,12,192,256]{3,2,1,0:T(8,128)S(1)}, f32[1,12,192,256]{3,2,1,0:T(8,128)S(1)}) fusion(f32[14,194,258]{2,1,0:T(8,128)S(1)} %fusion.3, f32[12,192,256]{2,1,0:T(8,128)S(1)} %fusion.20, f32[12,192,256]{2,1,0:T(8,128)S(1)} %get-tuple-element.26), kind=kLoop, calls=%fused_computation.63 | loop fusion | flops 8847360 | bytes 18874368 | tf_op jit(solution)/shard_map/stack | solution.py:117
  176.0 1.9 collective-permute-start.6
  177.9 7.6 %collective-permute-start.5 = (f32[3,1,192,256]{3,2,1,0:T(8,128)S(1)}, f32[3,1,192,256]{3,2,1,0:T(8,128)S(1)}, u32[]{:S(2)}, u32[]{:S(2)}) collective-permute-start(f32[3,1,192,256]{3,2,1,0:T(8,128)S(1)} %get-tuple-element.30), channel_id=1, source_target_pairs={{1,0},{2,1},{3,2},{4,3},{5,4},{6,5},{7,6},{8,7},{9,8},{10,9},{11,1... | collective-permute-start | bytes 1769480 | tf_op jit(solution)/shard_map/ppermute | solution.py:34
  185.6 5.4 %collective-permute-done.6 = f32[3,1,192,256]{3,2,1,0:T(8,128)S(1)} collective-permute-done((f32[3,1,192,256]{3,2,1,0:T(8,128)S(1)}, f32[3,1,192,256]{3,2,1,0:T(8,128)S(1)}, u32[]{:S(2)}, u32[]{:S(2)}) %collective-permute-start.6) | collective-permute-done | bytes 589856 | tf_op jit(solution)/shard_map/ppermute | solution.py:32
  193.6 9.4 %select_maximum_fusion = f32[3,14,194,258]{3,2,1,0:T(8,128)S(1)} fusion(f32[3,1,192,256]{3,2,1,0:T(8,128)S(1)} %collective-permute-done.5, f32[3,1,192,256]{3,2,1,0:T(8,128)S(1)} %collective-permute-done.6, f32[1,12,192,256]{3,2,1,0:T(8,128)S(1)} %get-tuple-element.28, f32[1,12,192,256]{3,2,1,0:T(8,128)S(1)} %get-tuple-element.27, ...), kind=kLoop, calls=%fused_computation.4 | loop fusion | flops 44145864 | bytes 16666272 | tf_op jit(solution)/shard_map/concatenate | solution.py:30
  203.0 7.0 %fusion.11 = f32[12,192,256]{2,1,0:T(8,128)} fusion(f32[12,192,256]{2,1,0:T(8,128)S(1)} %fusion.20, f32[3,14,194,258]{3,2,1,0:T(8,128)S(1)} %select_maximum_fusion, f32[3,1,192,256]{3,2,1,0:T(8,128)} %copy-done.4, f32[1,12,192,256]{3,2,1,0:T(8,128)S(1)} %get-tuple-element.28, f32[1,12,192,256]{3,2,1,0:T(8,128)S(1)} %get-tuple-element.27, ...), kind=kLoop, calls=%fused_computation.35 | loop fusion | flops 14745600 | bytes 24772608 | tf_op jit(solution)/shard_map/sub | solution.py:122
  211.1 1.9 collective-permute-start.7
  213.0 7.4 %collective-permute-start.8 = (f32[1,192,256]{2,1,0:T(8,128)S(1)}, f32[1,192,256]{2,1,0:T(8,128)S(1)}, u32[]{:S(2)}, u32[]{:S(2)}) collective-permute-start(f32[1,192,256]{2,1,0:T(8,128)S(1)} %get-tuple-element.35), channel_id=1, source_target_pairs={{1,0},{2,1},{3,2},{4,3},{5,4},{6,5},{7,6},{8,7},{9,8},{10,9},{11,1... | collective-permute-start | bytes 589832 | tf_op jit(solution)/shard_map/ppermute | solution.py:34
  221.9 1.8 collective-permute-done.8
  223.6 4.1 %select_maximum_fusion.4 = f32[14,194,258]{2,1,0:T(8,128)S(1)} fusion(f32[1,192,256]{2,1,0:T(8,128)S(1)} %collective-permute-done.8, f32[12,192,256]{2,1,0:T(8,128)} %fusion.11, f32[1,192,256]{2,1,0:T(8,128)S(1)} %collective-permute-done.7), kind=kLoop, calls=%fused_computation.19 | loop fusion | flops 10510920 | bytes 5555424 | tf_op jit(solution)/shard_map/concatenate | solution.py:30
  227.8 2.5 fusion.66
  230.2 1.9 fusion.25
  233.8 3.2 %reshape.200 = f32[6,96,2,258]{3,2,1,0:T(2,128)} reshape(f32[6,192,258]{2,1,0:T(8,128)} %get-tuple-element.40) | data formatting | bytes 2377728 | tf_op jit(solution)/shard_map/reshape | solution.py:62
  237.0 2.3 reshape.202
  240.3 3.9 %fusion.38 = f32[6,96,1,258]{3,2,1,0:T(1,128)S(1)} fusion(f32[6,96,2,258]{3,2,1,0:T(2,128)} %reshape.202, f32[6,96,2,258]{3,2,1,0:T(2,128)S(1)} %reshape.201, f32[6,96,2,258]{3,2,1,0:T(2,128)} %reshape.200), kind=kLoop, calls=%fused_computation.92 | loop fusion | flops 891648 | bytes 2972160 | tf_op jit(solution)/shard_map/add | solution.py:69
  (50 shorter events, 27.1 us)
Async XLA Ops:
  6.5 2.4 copy-start
  6.5 109.3 %all-reduce.6.cloned.1.call-start = ((), (), s32[]{:S(2)}) async-start(), calls=%async_computation | async-start | bytes 786432 | tf_op jit(solution)/shard_map/psum | solution.py:152
  18.6 2.9 %copy-start.3 = (f32[24,192,256]{2,1,0:T(8,128)}, f32[24,192,256]{2,1,0:T(8,128)S(1)}, u32[]{:S(2)}) copy-start(f32[24,192,256]{2,1,0:T(8,128)S(1)} %convolution_bitcast_fusion) | copy-start | bytes 14155780
  18.6 4.8 %copy-start.6 = (f32[1,6,96,128]{3,2,1,0:T(8,128)S(1)}, f32[1,6,96,128]{3,2,1,0:T(8,128)}, u32[]{:S(2)}) copy-start(f32[1,6,96,128]{3,2,1,0:T(8,128)} %param.9) | copy-start | bytes 884740
  21.5 126.1 %collective-permute-start.2 = (f32[12,192,256]{2,1,0:T(8,128)}, f32[12,192,256]{2,1,0:T(8,128)}, u32[]{:S(2)}, u32[]{:S(2)}) collective-permute-start(f32[12,192,256]{2,1,0:T(8,128)} %slice.263), channel_id=1, source_target_pairs={{0,1},{1,2},{2,3},{3,4},{4,5},{5,6},{6,7},{7,8},{8,9},{9,10},{10,1... | collective-permute-start | bytes 7077896 | tf_op jit(solution)/shard_map/ppermute | solution.py:21
  116.7 9.4 %collective-permute-start = (f32[1,96,128]{1,2,0:T(8,128)S(1)}, f32[1,96,128]{1,2,0:T(8,128)S(1)}, u32[]{:S(2)}, u32[]{:S(2)}) collective-permute-start(f32[1,96,128]{1,2,0:T(8,128)S(1)} %get-tuple-element.50), channel_id=1, source_target_pairs={{0,1},{1,2},{2,3},{3,4},{4,5},{5,6},{6,7},{7,8},{8,9},{9,10},{10,1... | collective-permute-start | bytes 147464 | tf_op jit(solution)/shard_map/ppermute | solution.py:32
  118.6 9.1 %collective-permute-start.1 = (f32[1,96,128]{1,2,0:T(8,128)S(1)}, f32[1,96,128]{1,2,0:T(8,128)S(1)}, u32[]{:S(2)}, u32[]{:S(2)}) collective-permute-start(f32[1,96,128]{1,2,0:T(8,128)S(1)} %get-tuple-element.51), channel_id=1, source_target_pairs={{1,0},{2,1},{3,2},{4,3},{5,4},{6,5},{7,6},{8,7},{9,8},{10,9},{11,1... | collective-permute-start | bytes 147464 | tf_op jit(solution)/shard_map/ppermute | solution.py:34
  150.4 10.7 %collective-permute-start.3 = (f32[1,1,192,256]{3,2,1,0:T(8,128)S(1)}, f32[1,1,192,256]{3,2,1,0:T(8,128)S(1)}, u32[]{:S(2)}, u32[]{:S(2)}) collective-permute-start(f32[1,1,192,256]{3,2,1,0:T(8,128)S(1)} %get-tuple-element.36), channel_id=1, source_target_pairs={{0,1},{1,2},{2,3},{3,4},{4,5},{5,6},{6,7},{7,8},{8,9},{9,10},{10,1... | collective-permute-start | bytes 589832 | tf_op jit(solution)/shard_map/ppermute | solution.py:32
  152.4 10.5 %collective-permute-start.4 = (f32[1,1,192,256]{3,2,1,0:T(8,128)S(1)}, f32[1,1,192,256]{3,2,1,0:T(8,128)S(1)}, u32[]{:S(2)}, u32[]{:S(2)}) collective-permute-start(f32[1,1,192,256]{3,2,1,0:T(8,128)S(1)} %get-tuple-element.37), channel_id=1, source_target_pairs={{1,0},{2,1},{3,2},{4,3},{5,4},{6,5},{7,6},{8,7},{9,8},{10,9},{11,1... | collective-permute-start | bytes 589832 | tf_op jit(solution)/shard_map/ppermute | solution.py:34
  171.4 4.4 %copy-start.2 = (f32[12,192,256]{2,1,0:T(8,128)}, f32[12,192,256]{2,1,0:T(8,128)S(1)}, u32[]{:S(2)}) copy-start(f32[12,192,256]{2,1,0:T(8,128)S(1)} %get-tuple-element.26) | copy-start | bytes 7077892
  176.0 15.0 %collective-permute-start.6 = (f32[3,1,192,256]{3,2,1,0:T(8,128)S(1)}, f32[3,1,192,256]{3,2,1,0:T(8,128)S(1)}, u32[]{:S(2)}, u32[]{:S(2)}) collective-permute-start(f32[3,1,192,256]{3,2,1,0:T(8,128)S(1)} %get-tuple-element.29), channel_id=1, source_target_pairs={{0,1},{1,2},{2,3},{3,4},{4,5},{5,6},{6,7},{7,8},{8,9},{9,10},{10,1... | collective-permute-start | bytes 1769480 | tf_op jit(solution)/shard_map/ppermute | solution.py:32
  177.9 14.8 %collective-permute-start.5 = (f32[3,1,192,256]{3,2,1,0:T(8,128)S(1)}, f32[3,1,192,256]{3,2,1,0:T(8,128)S(1)}, u32[]{:S(2)}, u32[]{:S(2)}) collective-permute-start(f32[3,1,192,256]{3,2,1,0:T(8,128)S(1)} %get-tuple-element.30), channel_id=1, source_target_pairs={{1,0},{2,1},{3,2},{4,3},{5,4},{6,5},{7,6},{8,7},{9,8},{10,9},{11,1... | collective-permute-start | bytes 1769480 | tf_op jit(solution)/shard_map/ppermute | solution.py:34
  191.0 1.8 copy-start.4
  192.7 0.8 copy-start.5
  211.1 10.8 %collective-permute-start.7 = (f32[1,192,256]{2,1,0:T(8,128)S(1)}, f32[1,192,256]{2,1,0:T(8,128)S(1)}, u32[]{:S(2)}, u32[]{:S(2)}) collective-permute-start(f32[1,192,256]{2,1,0:T(8,128)S(1)} %get-tuple-element.34), channel_id=1, source_target_pairs={{0,1},{1,2},{2,3},{3,4},{4,5},{5,6},{6,7},{7,8},{8,9},{9,10},{10,1... | collective-permute-start | bytes 589832 | tf_op jit(solution)/shard_map/ppermute | solution.py:32
  213.0 10.6 %collective-permute-start.8 = (f32[1,192,256]{2,1,0:T(8,128)S(1)}, f32[1,192,256]{2,1,0:T(8,128)S(1)}, u32[]{:S(2)}, u32[]{:S(2)}) collective-permute-start(f32[1,192,256]{2,1,0:T(8,128)S(1)} %get-tuple-element.35), channel_id=1, source_target_pairs={{1,0},{2,1},{3,2},{4,3},{5,4},{6,5},{7,6},{8,7},{9,8},{10,9},{11,1... | collective-permute-start | bytes 589832 | tf_op jit(solution)/shard_map/ppermute | solution.py:34
  244.9 2.2 copy-start.1
Sparse Core Ops, SparseCore 0:
  24.5 91.2 all-reduce.5
where the time goes:
time: 255 us; the launch traced here: 254 us
  waiting for transfers between devices  107 us (42%)
  other arithmetic  48.6 us (19%)
  starting transfers between devices  39.4 us (15%)
  local copies, waits for them, and re-layouts  36.1 us (14%)
  between operations  14.5 us (6%)
  matrix products  8.73 us (3%)
    psum x1, waiting for transfers between devices, body(): coarse = lax.psum(partial_density, 'band')[0]  91.4 us
    ppermute x4, starting transfers between devices, extended_2(): lax.ppermute(head, axis, [((i + 1) % count, i) for i in range(ends)])  29.8 us
    concatenate x3, other arithmetic, extended_2(): jnp.concatenate([lax.ppermute(tail, axis, [(i, (i + 1) % count) for i in...  14.8 us
    another operation x3, other arithmetic, transform(): jnp.stack([2.0 * by_sigma * grad_x, 2.0 * by_sigma * grad_y, 2.0 * by_sig...  10.5 us
    reshape x3, local copies, waits for them, and re-layouts, refine(): return joined.reshape(target)  8.89 us
    ppermute x4, waiting for transfers between devices, extended_2(): lax.ppermute(tail, axis, [(i, (i + 1) % count) for i in range(ends)])  8.23 us
    ppermute x4, starting transfers between devices, extended_2(): lax.ppermute(tail, axis, [(i, (i + 1) % count) for i in range(ends)])  7.68 us
    sub x1, other arithmetic, transform(): fine_potential = by_density - spread * half_inverse  7.04 us
  transfers between devices with their start and end apart: 10, of which 8 were waited for; matrix products, arithmetic and copies ran while one was open for 8% of the time, Pallas kernels for 0%

commit v1 on v0

v1 whole, which is shorter than its diff:
```python
import functools

import jax
import jax.numpy as jnp
from jax import lax
from jax.experimental import pallas as pl
from jax.experimental.pallas import tpu as pltpu
from jax.sharding import PartitionSpec as P

SLOTS = 8
SBX = 12
SBY = 24
SBZ = 24
CX = 6
FX = 12
RIM = 2
PARTS = 8
YB = 12
WY = 16
CZ = 128
FAR = -4096

KAPPA = 0.804
MU = 0.2195
PREFACTOR = -0.75 * (3.0 / 3.141592653589793) ** (1.0 / 3.0)
SCALE = 4.0 * (3.0 * 3.141592653589793**2) ** (2.0 / 3.0)
HALF_INVERSE = 0.5 / 0.2
DAMP = MU / KAPPA * HALF_INVERSE**2 / SCALE
B0 = PREFACTOR * 4.0 / 3.0 * (1.0 + KAPPA)
B1 = PREFACTOR * -4.0 * KAPPA
B2 = PREFACTOR * 8.0 / 3.0 * KAPPA
FLUX = 2.0 * HALF_INVERSE**2 * PREFACTOR * MU / SCALE


def place_kernel(meta, blocks, out, send_core, send_chip, total):
    for odd_z in range(2):
        total[odd_z, pl.ds(12, 12), pl.ds(24, 32), :] = jnp.zeros((12, 32, 128), jnp.float32)
    column = lax.broadcasted_iota(jnp.int32, (128, 256), 1)
    fine_z = jnp.where(column < 128, 2 * column, 2 * column - 255)
    inner_z = fine_z - lax.broadcasted_iota(jnp.int32, (128, 256), 0)
    row_z = lax.broadcasted_iota(jnp.int32, (128, 256), 0) < SBZ
    first_row = meta[48]
    for source in range(2):

        def one(slot, carry):
            row = meta[source * 24 + slot]
            col = meta[source * 24 + 8 + slot] - first_row + 24
            depth = meta[source * 24 + 16 + slot]

            @pl.when((col > 0) & (col < 56))
            def _():
                shift = lax.rem(col, 8)
                base = pl.multiple_of(col - shift, 8)
                block = blocks[source * SLOTS + slot]
                block = pltpu.roll(block, shift, 1).reshape(SBX * 32, 128)
                high = block.astype(jnp.bfloat16)
                low = (block - high.astype(jnp.float32)).astype(jnp.bfloat16)
                pick = jnp.where((inner_z == depth) & row_z, 1.0, 0.0).astype(jnp.bfloat16)
                spread = jnp.dot(high, pick, preferred_element_type=jnp.float32)
                spread = spread + jnp.dot(low, pick, preferred_element_type=jnp.float32)
                planes = pl.ds(row + 12 * (1 - source), SBX)
                rows = pl.ds(base, 32)
                spread = spread.reshape(SBX, 32, 256)
                for odd_z in range(2):
                    half = spread[:, :, 128 * odd_z : 128 * odd_z + 128]
                    total[odd_z, planes, rows, :] = total[odd_z, planes, rows, :] + half

            return carry

        lax.fori_loop(0, SLOTS, one, 0)
    for plane in range(12):
        for odd_y in range(2):
            for odd_z in range(2):
                rows = pl.ds(24 + odd_y, WY, stride=2)
                out[plane, odd_y, odd_z] = total[odd_z, plane + 12, rows, :]
    upper = meta[49] == 0

    @pl.when(upper)
    def _():
        send_core[...] = out[9:12]
        send_chip[...] = out[0:3]

    @pl.when(jnp.logical_not(upper))
    def _():
        send_core[...] = out[0:3]
        send_chip[...] = out[9:12]


def main_kernel(place, own, core, chip, dots, dots_core, dots_chip, out, dens, flux_x, value):
    slab = place[0]
    part = place[1]
    last = place[2]
    even_slab = lax.rem(slab, 2) == 0
    lane = lax.broadcasted_iota(jnp.int32, (WY, CZ), 1)
    first_lane = lane == 0
    last_lane = lane == CZ - 1
    row = lax.broadcasted_iota(jnp.int32, (WY, CZ), 0) + (YB * part - RIM)
    inside = (row >= 0) & (row < PARTS * YB)

    def row_before(x):
        return pltpu.roll(x, 1, 0)

    def row_after(x):
        return pltpu.roll(x, WY - 1, 0)

    def lane_before(x):
        return jnp.where(first_lane, 0.0, pltpu.roll(x, 1, 1))

    def lane_after(x):
        return jnp.where(last_lane, 0.0, pltpu.roll(x, CZ - 1, 1))

    def coarse(index):
        if index < 0:
            return jnp.where(even_slab, chip[index + 2], core[index + 2])
        if index >= CX:
            return jnp.where(even_slab, core[index - CX], chip[index - CX])
        return own[index]

    def spread(cells):
        middle = 0.75 * cells
        rows = [middle + 0.25 * row_before(cells), middle + 0.25 * row_after(cells)]
        result = []
        for cells_y in rows:
            middle = 0.75 * cells_y
            result.append(
                [middle + 0.25 * lane_before(cells_y), middle + 0.25 * lane_after(cells_y)]
            )
        return result

    def sphere(plane, odd_y, odd_z):
        if plane < 0:
            return jnp.where(
                even_slab, dots_chip[plane + 3, odd_y, odd_z], dots_core[plane + 3, odd_y, odd_z]
            )
        if plane >= FX:
            return jnp.where(
                even_slab, dots_core[plane - FX, odd_y, odd_z], dots_chip[plane - FX, odd_y, odd_z]
            )
        return dots[plane, odd_y, odd_z]

    def in_grid(plane):
        if plane < 0:
            return slab > 0
        if plane >= FX:
            return slab < last
        return None

    grids = {}
    for plane in range(-3, FX + 3):
        index, odd = plane // 2, plane % 2
        near = index + (1 if odd else -1)
        for which in (index, near):
            if which not in grids:
                grids[which] = spread(coarse(which))
        for old in [k for k in grids if k < min(index, near) - 1]:
            del grids[old]
        there = in_grid(plane)
        ok = inside if there is None else inside & there
        for odd_y in range(2):
            for odd_z in range(2):
                cells = 0.75 * grids[index][odd_y][odd_z] + 0.25 * grids[near][odd_y][odd_z]
                cells = cells + sphere(plane, odd_y, odd_z)
                dens[plane + 3, odd_y, odd_z] = jnp.where(ok, cells, 0.0)

    def density(plane):
        return [[dens[plane + 3, odd_y, odd_z] for odd_z in range(2)] for odd_y in range(2)]

    def differences(field_y, field_z):
        along_y = [[None] * 2 for _ in range(2)]
        along_z = [[None] * 2 for _ in range(2)]
        for other in range(2):
            along_y[0][other] = field_y[1][other] - row_before(field_y[1][other])
            along_y[1][other] = row_after(field_y[0][other]) - field_y[0][other]
            along_z[other][0] = field_z[other][1] - lane_before(field_z[other][1])
            along_z[other][1] = lane_after(field_z[other][0]) - field_z[other][0]
        return along_y, along_z

    def store_flux(plane):
        there = in_grid(plane)
        ok = inside if there is None else inside & there
        here = density(plane)
        grad_y, grad_z = differences(here, here)
        flux_y = [[None] * 2 for _ in range(2)]
        flux_z = [[None] * 2 for _ in range(2)]
        by_density = [[None] * 2 for _ in range(2)]
        for odd_y in range(2):
            for odd_z in range(2):
                grad_x = dens[plane + 4, odd_y, odd_z] - dens[plane + 2, odd_y, odd_z]
                gy, gz = grad_y[odd_y][odd_z], grad_z[odd_y][odd_z]
                squared = grad_x * grad_x + gy * gy + gz * gz
                cells = jnp.where(ok, here[odd_y][odd_z], 1.0)
                inverse_root = jnp.exp(jnp.log(cells) * (-1.0 / 3.0))
                power_2 = inverse_root * inverse_root
                power_4 = power_2 * power_2
                inverse = 1.0 / (1.0 + DAMP * squared * (power_4 * power_4))
                by_density[odd_y][odd_z] = cells * power_2 * (B0 + inverse * (B1 + B2 * inverse))
                weight = jnp.where(ok, FLUX * power_4 * (inverse * inverse), 0.0)
                flux_x[plane + 2, odd_y, odd_z] = weight * grad_x
                flux_y[odd_y][odd_z] = weight * gy
                flux_z[odd_y][odd_z] = weight * gz
        if -1 <= plane <= FX:
            spread_y, spread_z = differences(flux_y, flux_z)
            for odd_y in range(2):
                for odd_z in range(2):
                    value[plane + 1, odd_y, odd_z] = by_density[odd_y][odd_z] - (
                        spread_y[odd_y][odd_z] + spread_z[odd_y][odd_z]
                    )

    for plane in range(-2, FX + 2):
        store_flux(plane)

    def potential(plane, odd_y, odd_z):
        there = in_grid(plane)
        ok = inside if there is None else inside & there
        cells = value[plane + 1, odd_y, odd_z] - (
            flux_x[plane + 3, odd_y, odd_z] - flux_x[plane + 1, odd_y, odd_z]
        )
        return jnp.where(ok, cells, 0.0)

    for index in range(CX):
        depth = [None, None]
        for odd_z in range(2):
            rows = []
            for odd_y in range(2):
                low = potential(2 * index - 1, odd_y, odd_z) + potential(2 * index + 2, odd_y, odd_z)
                mid = potential(2 * index, odd_y, odd_z) + potential(2 * index + 1, odd_y, odd_z)
                rows.append(0.125 * low + 0.375 * mid)
            depth[odd_z] = 0.125 * (row_before(rows[1]) + row_after(rows[0])) + 0.375 * (rows[0] + rows[1])
        cells = 0.125 * (lane_before(depth[1]) + lane_after(depth[0])) + 0.375 * (depth[0] + depth[1])
        out[index] = cells[RIM : RIM + YB]


SMEM = pl.BlockSpec(memory_space=pltpu.SMEM)
VMEM = pl.BlockSpec(memory_space=pltpu.VMEM)
F32 = jnp.float32


def place_spheres(meta, blocks):
    rows = jax.ShapeDtypeStruct((3, 2, 2, WY, CZ), F32)
    return pl.pallas_call(
        place_kernel,
        out_shape=(jax.ShapeDtypeStruct((FX, 2, 2, WY, CZ), F32), rows, rows),
        in_specs=[SMEM, VMEM],
        out_specs=(VMEM, VMEM, VMEM),
        scratch_shapes=[pltpu.VMEM((2, 36, 80, 128), F32)],
        compiler_params=pltpu.CompilerParams(vmem_limit_bytes=32 * 2**20),
        name="place_spheres",
    )(meta, blocks)


def potential_of(place, own, core, chip, dots, dots_core, dots_chip):
    return pl.pallas_call(
        main_kernel,
        out_shape=jax.ShapeDtypeStruct((CX, YB, CZ), F32),
        in_specs=[SMEM] + [VMEM] * 6,
        out_specs=VMEM,
        scratch_shapes=[
            pltpu.VMEM((FX + 6, 2, 2, WY, CZ), F32),
            pltpu.VMEM((FX + 4, 2, 2, WY, CZ), F32),
            pltpu.VMEM((FX + 2, 2, 2, WY, CZ), F32),
        ],
        compiler_params=pltpu.CompilerParams(vmem_limit_bytes=32 * 2**20),
        name="potential_of",
    )(place, own, core, chip, dots, dots_core, dots_chip)


def body(partial_density, moments, shape_functions, sphere_offsets, owned_count):
    slab = lax.axis_index("dom")
    part = lax.axis_index("band")
    slabs = lax.axis_size("dom")
    even_slab = lax.rem(slab, 2) == 0
    core_pairs = [(i, i ^ 1) for i in range(slabs)]
    chip_pairs = [(i, i + 1) for i in range(1, slabs - 1, 2)]
    chip_pairs = chip_pairs + [(j, i) for i, j in chip_pairs]

    live = jnp.arange(SLOTS) < owned_count[0]
    blocks = jnp.einsum(
        "ls,slk->sk",
        moments * live.astype(jnp.bfloat16)[None, :],
        shape_functions,
        preferred_element_type=F32,
    )
    offsets = jnp.stack(
        [sphere_offsets[0], jnp.where(live, sphere_offsets[1], FAR), sphere_offsets[2]]
    )
    packed = jnp.concatenate(
        [blocks, jnp.pad(offsets.T.astype(F32), ((0, 0), (0, 125)))], axis=1
    )
    before = lax.ppermute(packed, "dom", [(i, i + 1) for i in range(slabs - 1)])

    padded = jnp.pad(partial_density[0], ((0, 0), (RIM, RIM), (0, 0)))
    windows = jnp.stack([padded[:, YB * b : YB * b + WY] for b in range(PARTS)])
    own = lax.all_to_all(windows, "band", 0, 0).sum(0)

    size = SBX * SBY * SBZ
    cubes = jnp.concatenate([blocks, before[:, :size]]).reshape(2 * SLOTS, SBX, SBY, SBZ)
    cubes = jnp.pad(cubes, ((0, 0), (0, 0), (0, 32 - SBY), (0, 128 - SBZ)))
    before_offsets = before[:, size : size + 3].T.astype(jnp.int32)
    meta = jnp.concatenate(
        [
            offsets.reshape(-1),
            before_offsets.reshape(-1),
            (2 * YB * part - 2 * RIM)[None].astype(jnp.int32),
            lax.rem(slab, 2)[None].astype(jnp.int32),
        ]
    )
    dots, send_core, send_chip = place_spheres(meta, cubes)
    dots_core = lax.ppermute(send_core, "dom", core_pairs)
    dots_chip = lax.ppermute(send_chip, "dom", chip_pairs)

    core = lax.ppermute(jnp.where(even_slab, own[4:6], own[0:2]), "dom", core_pairs)
    chip = lax.ppermute(jnp.where(even_slab, own[0:2], own[4:6]), "dom", chip_pairs)
    place = jnp.stack([slab, part, jnp.int32(slabs - 1)]).astype(jnp.int32)
    result = potential_of(place, own, core, chip, dots, dots_core, dots_chip)
    copies = jnp.broadcast_to(result[None], (PARTS, CX, YB, CZ))
    gathered = lax.all_to_all(copies, "band", 0, 0)
    return gathered.transpose(1, 0, 2, 3).reshape(CX, PARTS * YB, CZ)


def solution(mesh):
    return jax.shard_map(
        body,
        mesh=mesh,
        in_specs=(
            P("band", "dom", None, None),
            P(None, "dom"),
            P("dom", None, None),
            P(None, "dom"),
            P("dom"),
        ),
        out_specs=P("dom", None, None),
        check_vma=False,
    )
```

time: 255 us -> 55.6 us (0.22)
  waiting for transfers between devices: 107 us -> 5.69 us
  other arithmetic: 48.6 us -> 2.88 us
  local copies, waits for them, and re-layouts: 36.1 us -> 10.3 us
  starting transfers between devices: 39.4 us -> 17.9 us
  blocking collectives: 0 us -> 14.1 us
  between operations: 14.5 us -> 0.91 us
  matrix products: 8.73 us -> 0.5 us
  Pallas kernels: 0 us -> 2.83 us
    psum x1 -> x0, waiting for transfers between devices: 91.4 us -> none  [body(): coarse = lax.psum(partial_density, 'band')[0]]
    ppermute x9 -> x5, starting transfers between devices: 39.4 us -> 12.8 us  [the longest x1 6.36 us: body(): dots_chip = lax.ppermute(send_chip, 'dom', chip_pairs)]
    all_to_all x0 -> x1, blocking collectives: none -> 14.1 us  [body(): gathered = lax.all_to_all(copies, 'band', 0, 0)]
    concatenate x3, other arithmetic: 14.8 us -> 0.91 us  [the longest x1 0.81 us: body(): jnp.concatenate([blocks, before[:, :size]])]
    another operation x9 -> x1, other arithmetic: 13.5 us -> 0.08 us  [body(): place = jnp.stack([slab, part, jnp.int32(slabs - 1)]).astype(jnp.int32)]
    reshape x7 -> x4, local copies, waits for them, and re-layouts: 16.2 us -> 3.63 us  [the longest x1 2.72 us: body(): jnp.concatenate([blocks, before[:, :size]])]
    add x6 -> x0, other arithmetic: 9.95 us -> none  [the longest x3 6.97 us: restrict(): 0.125 * outer_low + 0.375 * (first_half + second_half) + 0.125 * outer_high]
    ppermute x9 -> x5, waiting for transfers between devices: 15.2 us -> 5.69 us  [the longest x1 5.68 us: body(): lax.ppermute(jnp.where(even_slab, own[0:2], own[4:6]), 'dom', chip_pairs)]
  transfers between devices with their start and end apart: 10 -> 6, of which waited for: 8 -> 1; matrix products, arithmetic and copies ran while one was open for 8% -> 19% of each run, Pallas kernels for 0% -> 2%
where the time goes in v1:
time: 55.6 us; the launch traced here: 55.1 us
  starting transfers between devices  17.9 us (32%)
  blocking collectives  14.1 us (25%)
  local copies, waits for them, and re-layouts  10.3 us (19%)
  waiting for transfers between devices  5.69 us (10%)
  other arithmetic  2.88 us (5%)
  Pallas kernels  2.83 us (5%)
  between operations  0.91 us (2%)
    all_to_all x1, blocking collectives, body(): gathered = lax.all_to_all(copies, 'band', 0, 0)  14.1 us
    ppermute x1, starting transfers between devices, body(): dots_chip = lax.ppermute(send_chip, 'dom', chip_pairs)  6.36 us
    ppermute x1, waiting for transfers between devices, body(): lax.ppermute(jnp.where(even_slab, own[0:2], own[4:6]), 'dom', chip_pairs)  5.68 us
    all_to_all x1, starting transfers between devices, body(): own = lax.all_to_all(windows, 'band', 0, 0).sum(0)  5.1 us
    unnamed x14, local copies, waits for them, and re-layouts  4.58 us
    ppermute x1, starting transfers between devices, body(): lax.ppermute(jnp.where(even_slab, own[0:2], own[4:6]), 'dom', chip_pairs)  2.8 us
    reshape x1, local copies, waits for them, and re-layouts, body(): jnp.concatenate([blocks, before[:, :size]])  2.72 us
    ppermute x1, starting transfers between devices, body(): before = lax.ppermute(packed, 'dom', [(i, i + 1) for i in range(slabs - 1)])  1.92 us
  transfers between devices with their start and end apart: 6, of which 1 were waited for; matrix products, arithmetic and copies ran while one was open for 19% of the time, Pallas kernels for 2%

profile of v1, /device:TPU:4, one launch (start us, length us, event | category | flops | bytes accessed | tf_op | source)
XLA Modules:
  0.0 55.1 jit_solution(9780784256110310947)
XLA Ops:
  0.8 0.8 %fusion.15 = (s32[1,8]{1,0:T(1,128)S(1)}, s32[1,8]{1,0:T(1,128)S(1)}, s32[1,8]{1,0:T(1,128)S(1)}) fusion(s32[3,8]{1,0:T(4,128)} %param.8), kind=kLoop, calls=%fused_computation.37 | loop fusion | bytes 192 | tf_op jit(solution)/shard_map/slice | solution.py:284
  1.6 0.1 copy.17
  1.7 0.1 copy.18
  1.8 0.8 %multiply_bitcast_fusion = bf16[9,8,1]{0,1,2:T(8,128)(2,1)S(1)} fusion(bf16[9,8]{0,1:T(8,128)(2,1)} %param.6, bf16[8]{0:T(256)(128)(2,1)S(1)} %compare_convert_fusion), kind=kLoop, calls=%fused_computation.33 | loop fusion | flops 72 | bytes 304 | tf_op jit(solution)/shard_map/mul | solution.py:279
  2.6 0.5 fusion
  3.2 1.9 %collective-permute-start.2 = (f32[8,7040]{1,0:T(8,128)S(1)}, f32[8,7040]{1,0:T(8,128)S(1)}, u32[]{:S(2)}, u32[]{:S(2)}) collective-permute-start(f32[8,7040]{1,0:T(8,128)S(1)} %select_maximum_fusion), channel_id=1, source_target_pairs={{0,1},{1,2},{2,3},{3,4},{4,5},{5,6},{6,7},{7,8},{8,9},{9,10},{10,1... | collective-permute-start | bytes 675848 | tf_op jit(solution)/shard_map/ppermute | solution.py:289
  5.1 0.6 %fusion.3 = f32[8,6,16,128]{3,2,1,0:T(8,128)} fusion(f32[6,96,128]{2,1,0:T(8,128)S(1)} %bitcast.50), kind=kLoop, calls=%fused_computation.9 | loop fusion | bytes 344064
  5.8 0.6 %fusion.11 = f32[8,6,16,128]{3,2,1,0:T(8,128)} fusion(f32[8,6,16,128]{3,2,1,0:T(8,128)} %fusion.3, f32[6,96,128]{2,1,0:T(8,128)S(1)} %bitcast.51), kind=kLoop, calls=%fused_computation.23 | loop fusion | bytes 98304
  6.4 0.6 %fusion.10 = f32[8,6,16,128]{3,2,1,0:T(8,128)} fusion(f32[8,6,16,128]{3,2,1,0:T(8,128)} %fusion.11, f32[6,96,128]{2,1,0:T(8,128)S(1)} %bitcast.52), kind=kLoop, calls=%fused_computation.21 | loop fusion | bytes 98304
  7.0 0.6 %fusion.9 = f32[8,6,16,128]{3,2,1,0:T(8,128)} fusion(f32[8,6,16,128]{3,2,1,0:T(8,128)} %fusion.10, f32[6,96,128]{2,1,0:T(8,128)S(1)} %bitcast.53), kind=kLoop, calls=%fused_computation.19 | loop fusion | bytes 98304
  7.6 0.6 %fusion.8 = f32[8,6,16,128]{3,2,1,0:T(8,128)} fusion(f32[8,6,16,128]{3,2,1,0:T(8,128)} %fusion.9, f32[6,96,128]{2,1,0:T(8,128)S(1)} %bitcast.54), kind=kLoop, calls=%fused_computation.17 | loop fusion | bytes 98304
  8.2 0.6 %fusion.7 = f32[8,6,16,128]{3,2,1,0:T(8,128)} fusion(f32[8,6,16,128]{3,2,1,0:T(8,128)} %fusion.8, f32[6,96,128]{2,1,0:T(8,128)S(1)} %bitcast.55), kind=kLoop, calls=%fused_computation.15 | loop fusion | bytes 98304
  8.9 0.6 %fusion.6 = f32[8,6,16,128]{3,2,1,0:T(8,128)} fusion(f32[8,6,16,128]{3,2,1,0:T(8,128)} %fusion.7, f32[6,96,128]{2,1,0:T(8,128)S(1)} %bitcast.56), kind=kLoop, calls=%fused_computation.13 | loop fusion | bytes 98304
  9.5 0.6 %fusion.5 = f32[8,6,16,128]{3,2,1,0:T(8,128)} fusion(f32[8,6,16,128]{3,2,1,0:T(8,128)} %fusion.6, f32[6,96,128]{2,1,0:T(8,128)S(1)} %bitcast.57), kind=kLoop, calls=%fused_computation.11 | loop fusion | bytes 344064 | tf_op jit(solution)/shard_map/stack | solution.py:292
  10.1 5.1 %all-to-all-start = ((f32[8,6,16,128]{3,2,1,0:T(8,128)}), f32[8,6,16,128]{3,2,1,0:T(8,128)}, u32[]{:S(2)}, u32[]{:S(2)}) async-start(f32[8,6,16,128]{3,2,1,0:T(8,128)} %fusion.5), calls=%async_computation | async-start | bytes 786432 | tf_op jit(solution)/shard_map/all_to_all | solution.py:293
  15.3 0.1 reshape.23
  15.4 0.8 %pad_maximum_fusion = f32[16,6912]{1,0:T(8,128)} fusion(f32[8,6912]{1,0:T(8,128)S(1)} %slice.77, f32[8,6912]{1,0:T(8,128)S(1)} %bitcast.59), kind=kLoop, calls=%fused_computation.2 | loop fusion | flops 110592 | bytes 884736 | tf_op jit(solution)/shard_map/concatenate | solution.py:296
  16.2 0.1 copy.12
  16.3 0.1 reshape.24
  16.4 2.7 %reshape.25 = f32[16,12,24,24]{3,2,1,0:T(8,128)S(1)} reshape(f32[16,6912]{1,0:T(8,128)} %pad_maximum_fusion) | data formatting | bytes 884736 | tf_op jit(solution)/shard_map/reshape | solution.py:296
  19.1 0.4 pad.14.blocks
  19.5 0.1 pad_add_fusion.2.meta
  19.6 1.1 %place_spheres.1 = (f32[12,2,2,16,128]{4,3,2,1,0:T(8,128)S(1)}, f32[3,2,2,16,128]{4,3,2,1,0:T(8,128)S(1)}, f32[3,2,2,16,128]{4,3,2,1,0:T(8,128)S(1)}) custom-call(s32[50]{0:T(128)S(1)} %pad_add_fusion.2.meta, f32[16,12,32,128]{3,2,1,0:T(8,128)S(1)} %pad.14.blocks), custom_call_target="tpu_custom_call" | custom-call | tf_op jit(solution)/shard_map/place_spheres/pallas_call | solution.py:240
  20.8 1.6 %collective-permute-start.3 = (f32[3,2,2,16,128]{4,3,2,1,0:T(8,128)S(1)}, f32[3,2,2,16,128]{4,3,2,1,0:T(8,128)S(1)}, u32[]{:S(2)}, u32[]{:S(2)}) collective-permute-start(f32[3,2,2,16,128]{4,3,2,1,0:T(8,128)S(1)} %get-tuple-element.9), channel_id=1, source_target_pairs={{0,1},{1,0},{2,3},{3,2},{4,5},{5,4},{6,7},{7,6},{8,9},{9,8},{10,11... | collective-permute-start | bytes 294920 | tf_op jit(solution)/shard_map/ppermute | solution.py:308
  22.3 6.4 %collective-permute-start.4 = (f32[3,2,2,16,128]{4,3,2,1,0:T(8,128)S(1)}, f32[3,2,2,16,128]{4,3,2,1,0:T(8,128)S(1)}, u32[]{:S(2)}, u32[]{:S(2)}) collective-permute-start(f32[3,2,2,16,128]{4,3,2,1,0:T(8,128)S(1)} %get-tuple-element.10), channel_id=1, source_target_pairs={{1,2},{3,4},{5,6},{7,8},{9,10},{11,12},{13,14},{15,16},{17,18},{19... | collective-permute-start | bytes 294920 | tf_op jit(solution)/shard_map/ppermute | solution.py:309
  28.7 1.0 %reduce_sum.9.own = f32[6,16,128]{2,1,0:T(8,128)S(1)} reduce(f32[8,6,16,128]{3,2,1,0:T(8,128)} %all-to-all-done, f32[]{:T(128)} %constant.21.clone.1), dimensions={0}, to_apply=%region_0.1 | reduce | flops 86016 | bytes 442372 | tf_op jit(solution)/shard_map/reduce_sum | solution.py:293
  29.8 2.8 %collective-permute-start.1 = (f32[2,16,128]{2,1,0:T(8,128)S(1)}, f32[2,16,128]{2,1,0:T(8,128)S(1)}, u32[]{:S(2)}, u32[]{:S(2)}) collective-permute-start(f32[2,16,128]{2,1,0:T(8,128)S(1)} %get-tuple-element.13), channel_id=1, source_target_pairs={{1,2},{3,4},{5,6},{7,8},{9,10},{11,12},{13,14},{15,16},{17,18},{19... | collective-permute-start | bytes 49160 | tf_op jit(solution)/shard_map/ppermute | solution.py:312
  32.6 0.1 collective-permute-start
  32.8 5.7 %collective-permute-done.1.chip = f32[2,16,128]{2,1,0:T(8,128)S(1)} collective-permute-done((f32[2,16,128]{2,1,0:T(8,128)S(1)}, f32[2,16,128]{2,1,0:T(8,128)S(1)}, u32[]{:S(2)}, u32[]{:S(2)}) %collective-permute-start.1) | collective-permute-done | bytes 16416 | tf_op jit(solution)/shard_map/ppermute | solution.py:312
  38.4 1.7 %potential_of.1 = f32[6,12,128]{2,1,0:T(8,128)S(1)} custom-call(s32[3]{0:T(128)S(1)} %pad_add_fusion.1.place, f32[6,16,128]{2,1,0:T(8,128)S(1)} %reduce_sum.9.own, f32[2,16,128]{2,1,0:T(8,128)S(1)} %collective-permute-done.core, f32[2,16,128]{2,1,0:T(8,128)S(1)} %collective-permute-done.1.chip, f32[12,2,2,16,128]{4,3,2,1,0:T(8,128)S(1)} %get-tuple-element.8.dots, ...), custom_call_target="tpu_custom_call" | custom-call | tf_op jit(solution)/shard_map/potential_of/pallas_call | solution.py:252
  40.2 14.1 %all_to_all.10 = f32[8,6,12,128]{3,2,1,0:T(8,128)S(1)} all-to-all(f32[8,6,12,128]{3,2,1,0:T(8,128)S(1)} %broadcast_in_dim.20), channel_id=1, replica_groups=mesh['band'=8,'dom'=32] {'band'}, dimensions={0} | all-to-all | bytes 589824 | tf_op jit(solution)/shard_map/all_to_all | solution.py:316
  54.3 0.7 %reshape.26 = f32[6,96,128]{2,1,0:T(8,128)} reshape(f32[6,8,12,128]{3,2,1,0:T(8,128)S(1)} %copy.13) | data formatting | bytes 589824 | tf_op jit(solution)/shard_map/reshape | solution.py:317
  (22 shorter events, 0.5 us)
Async XLA Ops:
  0.0 2.6 %copy-start = (bf16[8,9,6912]{2,0,1:T(8,128)(2,1)S(1)}, bf16[8,9,6912]{2,0,1:T(8,128)(2,1)}, u32[]{:S(2)}) copy-start(bf16[8,9,6912]{2,0,1:T(8,128)(2,1)} %param.7) | copy-start | bytes 2985988
  0.0 5.1 %copy-start.1 = (f32[1,6,96,128]{3,2,1,0:T(8,128)S(1)}, f32[1,6,96,128]{3,2,1,0:T(8,128)}, u32[]{:S(2)}) copy-start(f32[1,6,96,128]{3,2,1,0:T(8,128)} %param.5) | copy-start | bytes 884740
  3.2 12.2 %collective-permute-start.2 = (f32[8,7040]{1,0:T(8,128)S(1)}, f32[8,7040]{1,0:T(8,128)S(1)}, u32[]{:S(2)}, u32[]{:S(2)}) collective-permute-start(f32[8,7040]{1,0:T(8,128)S(1)} %select_maximum_fusion), channel_id=1, source_target_pairs={{0,1},{1,2},{2,3},{3,4},{4,5},{5,6},{6,7},{7,8},{8,9},{9,10},{10,1... | collective-permute-start | bytes 675848 | tf_op jit(solution)/shard_map/ppermute | solution.py:289
  10.1 18.6 %all-to-all-start = ((f32[8,6,16,128]{3,2,1,0:T(8,128)}), f32[8,6,16,128]{3,2,1,0:T(8,128)}, u32[]{:S(2)}, u32[]{:S(2)}) async-start(f32[8,6,16,128]{3,2,1,0:T(8,128)} %fusion.5), calls=%async_computation | async-start | bytes 786432 | tf_op jit(solution)/shard_map/all_to_all | solution.py:293
  20.8 12.0 %collective-permute-start.3 = (f32[3,2,2,16,128]{4,3,2,1,0:T(8,128)S(1)}, f32[3,2,2,16,128]{4,3,2,1,0:T(8,128)S(1)}, u32[]{:S(2)}, u32[]{:S(2)}) collective-permute-start(f32[3,2,2,16,128]{4,3,2,1,0:T(8,128)S(1)} %get-tuple-element.9), channel_id=1, source_target_pairs={{0,1},{1,0},{2,3},{3,2},{4,5},{5,4},{6,7},{7,6},{8,9},{9,8},{10,11... | collective-permute-start | bytes 294920 | tf_op jit(solution)/shard_map/ppermute | solution.py:308
  22.3 10.4 %collective-permute-start.4 = (f32[3,2,2,16,128]{4,3,2,1,0:T(8,128)S(1)}, f32[3,2,2,16,128]{4,3,2,1,0:T(8,128)S(1)}, u32[]{:S(2)}, u32[]{:S(2)}) collective-permute-start(f32[3,2,2,16,128]{4,3,2,1,0:T(8,128)S(1)} %get-tuple-element.10), channel_id=1, source_target_pairs={{1,2},{3,4},{5,6},{7,8},{9,10},{11,12},{13,14},{15,16},{17,18},{19... | collective-permute-start | bytes 294920 | tf_op jit(solution)/shard_map/ppermute | solution.py:309
  29.8 8.7 %collective-permute-start.1 = (f32[2,16,128]{2,1,0:T(8,128)S(1)}, f32[2,16,128]{2,1,0:T(8,128)S(1)}, u32[]{:S(2)}, u32[]{:S(2)}) collective-permute-start(f32[2,16,128]{2,1,0:T(8,128)S(1)} %get-tuple-element.13), channel_id=1, source_target_pairs={{1,2},{3,4},{5,6},{7,8},{9,10},{11,12},{13,14},{15,16},{17,18},{19... | collective-permute-start | bytes 49160 | tf_op jit(solution)/shard_map/ppermute | solution.py:312
  32.6 5.9 %collective-permute-start = (f32[2,16,128]{2,1,0:T(8,128)S(1)}, f32[2,16,128]{2,1,0:T(8,128)S(1)}, u32[]{:S(2)}, u32[]{:S(2)}) collective-permute-start(f32[2,16,128]{2,1,0:T(8,128)S(1)} %get-tuple-element.14), channel_id=1, source_target_pairs={{0,1},{1,0},{2,3},{3,2},{4,5},{5,4},{6,7},{7,6},{8,9},{9,8},{10,11... | collective-permute-start | bytes 49160 | tf_op jit(solution)/shard_map/ppermute | solution.py:311

commit v2 on v1

v2 whole, which is shorter than its diff:
```python
import jax
import jax.numpy as jnp
from jax import lax
from jax.experimental import pallas as pl
from jax.experimental.pallas import tpu as pltpu
from jax.sharding import PartitionSpec as P

SLOTS = 8
SBX = 12
SBY = 24
SBZ = 24
BLOCK = SBX * SBY * SBZ
NL = 9
TAIL = 2 * SBY * SBZ + 128
CX = 6
FX = 12
RIM = 2
PARTS = 8
YB = 12
WY = 16
CZ = 128
FAR = -4096

KAPPA = 0.804
MU = 0.2195
PREFACTOR = -0.75 * (3.0 / 3.141592653589793) ** (1.0 / 3.0)
SCALE = 4.0 * (3.0 * 3.141592653589793**2) ** (2.0 / 3.0)
HALF_INVERSE = 0.5 / 0.2
DAMP = MU / KAPPA * HALF_INVERSE**2 / SCALE
B0 = PREFACTOR * 4.0 / 3.0 * (1.0 + KAPPA)
B1 = PREFACTOR * -4.0 * KAPPA
B2 = PREFACTOR * 8.0 / 3.0 * KAPPA
FLUX = 2.0 * HALF_INVERSE**2 * PREFACTOR * MU / SCALE


def windows_kernel(cells, windows, held, sems):
    copies = []
    for third in range(3):
        planes = pl.ds(2 * third, 2)
        copies.append(pltpu.make_async_copy(cells.at[0, planes], held.at[planes], sems.at[third]))
        copies[-1].start()
    for third in range(3):
        copies[third].wait()
        planes = pl.ds(2 * third, 2)
        for part in range(PARTS):
            first = YB * part - RIM
            low, high = max(first, 0), min(first + WY, PARTS * YB)
            rows = held[planes, low:high, :]
            if low > first:
                rows = jnp.concatenate([jnp.zeros((2, low - first, CZ), jnp.float32), rows], axis=1)
            if high < first + WY:
                rows = jnp.concatenate([rows, jnp.zeros((2, first + WY - high, CZ), jnp.float32)], axis=1)
            windows[part, planes] = rows


def blocks_kernel(offsets, count, moments, shapes, packed, tail, held, sems):
    step = BLOCK // 3
    copies = []
    for third in range(3):
        lanes = pl.ds(step * third, step)
        copies.append(
            pltpu.make_async_copy(shapes.at[:, :, lanes], held.at[:, :, lanes], sems.at[third])
        )
        copies[-1].start()
    row = lax.broadcasted_iota(jnp.int32, (SLOTS, 128), 0)
    lane = lax.broadcasted_iota(jnp.int32, (SLOTS, 128), 1)
    info = jnp.zeros((SLOTS, 128), jnp.int32)
    for which in range(SLOTS):
        for dim in range(3):
            value = offsets[dim, which]
            if dim == 1:
                value = jnp.where(which < count[0], value, FAR)
            info = jnp.where((row == which) & (lane == dim), value, info)
    packed[:, BLOCK : BLOCK + 128] = info.astype(jnp.float32)
    slot = lax.broadcasted_iota(jnp.int32, (SLOTS, 1), 0)
    weights = jnp.where(slot < count[0], moments[...].astype(jnp.float32), 0.0)
    for third in range(3):
        copies[third].wait()
        for chunk in range(3):
            lanes = pl.ds(step * third + chunk * (step // 3), step // 3)
            total = weights[:, 0:1] * held[0, :, lanes].astype(jnp.float32)
            for channel in range(1, NL):
                total = total + weights[:, channel : channel + 1] * held[channel, :, lanes].astype(
                    jnp.float32
                )
            packed[:, lanes] = total
    tail[...] = packed[:, BLOCK + 128 - TAIL :]


def spread_blocks(sources, flat, total):
    lane = lax.broadcasted_iota(jnp.int32, (SLOTS, 128), 1)
    for read, depth_x, _, begin, _, _ in sources:
        tiles = {}
        for line in range(depth_x * SBY):
            tile, skip = divmod(line * SBZ, 128)
            for needed in (tile, tile + 1) if skip + SBZ > 128 else (tile,):
                if needed not in tiles:
                    tiles = {k: v for k, v in tiles.items() if k >= tile}
                    tiles[needed] = read(needed)
            cells = tiles[tile]
            if skip + SBZ > 128:
                cells = jnp.where(lane >= skip, cells, tiles[tile + 1])
            if skip:
                cells = pltpu.roll(cells, 128 - skip, 1)
            flat[pl.ds(64 + SLOTS * (begin * SBY + line), SLOTS), :] = jnp.where(lane < SBZ, cells, 0.0)
    column = lax.broadcasted_iota(jnp.int32, (128, 256), 1)
    fine_z = jnp.where(column < 128, 2 * column, 2 * column - 255)
    inner_z = fine_z - lax.broadcasted_iota(jnp.int32, (128, 256), 0)
    row_z = lax.broadcasted_iota(jnp.int32, (128, 256), 0) < SBZ
    row_y = lax.broadcasted_iota(jnp.int32, (32, 128), 0)
    first_row = 2 * (YB * lax.axis_index("band") - RIM)
    for _, depth_x, first_plane, begin, value, there in sources:

        def one(slot, carry):
            row = value(slot, 0)
            col = value(slot, 1) - first_row + 24
            depth = value(slot, 2)
            meets = (col > 0) & (col < 56)

            @pl.when(meets if there is None else meets & there)
            def _():
                shift = lax.rem(col, 8)
                base = pl.multiple_of(col - shift, 8)
                held = (row_y >= shift) & (row_y < shift + SBY)
                parts = []
                for x in range(depth_x):
                    start = 64 + ((begin + x) * SBY - shift) * SLOTS + slot
                    parts.append(jnp.where(held, flat[pl.ds(start, 32, stride=SLOTS), :], 0.0))
                block = jnp.concatenate(parts, axis=0)
                high = block.astype(jnp.bfloat16)
                low = (block - high.astype(jnp.float32)).astype(jnp.bfloat16)
                pick = jnp.where((inner_z == depth) & row_z, 1.0, 0.0).astype(jnp.bfloat16)
                spread = jnp.dot(high, pick, preferred_element_type=jnp.float32)
                spread = spread + jnp.dot(low, pick, preferred_element_type=jnp.float32)
                planes = pl.ds(row + first_plane, depth_x)
                rows = pl.ds(base, 32)
                spread = spread.reshape(depth_x, 32, 256)
                for odd_z in range(2):
                    half = spread[:, :, 128 * odd_z : 128 * odd_z + 128]
                    total[odd_z, planes, rows, :] = total[odd_z, planes, rows, :] + half

            return carry

        lax.fori_loop(0, SLOTS, one, 0)


def place_own_kernel(offsets, count, own, out, flat, total):
    for odd_z in range(2):
        total[odd_z, pl.ds(11, 18), pl.ds(24, 32), :] = jnp.zeros((18, 32, 128), jnp.float32)

    def read(tile):
        return own[:, 128 * tile : 128 * tile + 128]

    def value(slot, which):
        if which == 1:
            return jnp.where(slot < count[0], offsets[1, slot], FAR)
        return offsets[which, slot]

    spread_blocks([(read, SBX, 14, 0, value, None)], flat, total)
    for odd_z in range(2):
        out[odd_z] = total[odd_z, pl.ds(11, 18), pl.ds(24, 32), :]


def place_kernel(own, core, chip, second, out, flat, total, info, sems):
    slab = lax.axis_index("dom")
    even_slab = lax.rem(slab, 2) == 0
    copies = []
    for index, (ref, start) in enumerate(
        ((core, BLOCK), (chip, BLOCK), (second, TAIL - 128))
    ):
        copies.append(
            pltpu.make_async_copy(ref.at[:, pl.ds(start, 128)], info.at[index], sems.at[index])
        )
        copies[-1].start()
    for odd_z in range(2):
        total[odd_z, pl.ds(11, 18), pl.ds(24, 32), :] = own[odd_z]

    def before_tile(tile):
        lanes = pl.ds(128 * tile, 128)
        return jnp.where(even_slab, chip[:, lanes], core[:, lanes])

    def after_tile(tile):
        lanes = pl.ds(128 * tile, 128)
        return jnp.where(even_slab, core[:, lanes], chip[:, lanes])

    def second_tile(tile):
        return second[:, 128 * tile : 128 * tile + 128]

    def value_of(if_even, if_odd):
        def value(slot, which):
            both = jnp.where(even_slab, info[if_even, slot, which], info[if_odd, slot, which])
            return both.astype(jnp.int32)

        return value

    for copy in copies:
        copy.wait()
    last = lax.axis_size("dom") - 1
    spread_blocks(
        [
            (before_tile, SBX, 2, 0, value_of(1, 0), slab > 0),
            (after_tile, 3, 26, SBX, value_of(0, 1), slab < last),
            (second_tile, 2, 0, SBX + 3, value_of(2, 2), slab > 1),
        ],
        flat,
        total,
    )
    for plane in range(FX + 6):
        for odd_y in range(2):
            for odd_z in range(2):
                rows = pl.ds(24 + odd_y, WY, stride=2)
                out[plane, odd_y, odd_z] = total[odd_z, plane + 11, rows, :]


def own_kernel(windows, own, send_core, send_chip):
    for plane in range(CX):
        cells = windows[0, plane]
        for part in range(1, PARTS):
            cells = cells + windows[part, plane]
        own[plane] = cells
    even_slab = lax.rem(lax.axis_index("dom"), 2) == 0
    send_core[...] = jnp.where(even_slab, own[CX - 2 : CX], own[0:2])
    send_chip[...] = jnp.where(even_slab, own[0:2], own[CX - 2 : CX])


def main_kernel(own, core, chip, dots, out, dens, flux_x, value):
    slab = lax.axis_index("dom")
    part = lax.axis_index("band")
    last = lax.axis_size("dom") - 1
    even_slab = lax.rem(slab, 2) == 0
    lane = lax.broadcasted_iota(jnp.int32, (WY, CZ), 1)
    first_lane = lane == 0
    last_lane = lane == CZ - 1
    row = lax.broadcasted_iota(jnp.int32, (WY, CZ), 0) + (YB * part - RIM)
    inside = (row >= 0) & (row < PARTS * YB)

    def row_before(x):
        return pltpu.roll(x, 1, 0)

    def row_after(x):
        return pltpu.roll(x, WY - 1, 0)

    def lane_before(x):
        return jnp.where(first_lane, 0.0, pltpu.roll(x, 1, 1))

    def lane_after(x):
        return jnp.where(last_lane, 0.0, pltpu.roll(x, CZ - 1, 1))

    def coarse(index):
        if index < 0:
            cells = jnp.where(even_slab, chip[index + 2], core[index + 2])
            return jnp.where(slab > 0, cells, 0.0)
        if index >= CX:
            cells = jnp.where(even_slab, core[index - CX], chip[index - CX])
            return jnp.where(slab < last, cells, 0.0)
        return own[index]

    def spread(cells):
        middle = 0.75 * cells
        rows = [middle + 0.25 * row_before(cells), middle + 0.25 * row_after(cells)]
        result = []
        for cells_y in rows:
            middle = 0.75 * cells_y
            result.append(
                [middle + 0.25 * lane_before(cells_y), middle + 0.25 * lane_after(cells_y)]
            )
        return result

    def in_grid(plane):
        if plane < 0:
            return slab > 0
        if plane >= FX:
            return slab < last
        return None

    grids = {}
    for plane in range(-3, FX + 3):
        index, odd = plane // 2, plane % 2
        near = index + (1 if odd else -1)
        for which in (index, near):
            if which not in grids:
                grids[which] = spread(coarse(which))
        for old in [k for k in grids if k < min(index, near) - 1]:
            del grids[old]
        there = in_grid(plane)
        ok = inside if there is None else inside & there
        for odd_y in range(2):
            for odd_z in range(2):
                cells = 0.75 * grids[index][odd_y][odd_z] + 0.25 * grids[near][odd_y][odd_z]
                cells = cells + dots[plane + 3, odd_y, odd_z]
                dens[plane + 3, odd_y, odd_z] = jnp.where(ok, cells, 0.0)

    def density(plane):
        return [[dens[plane + 3, odd_y, odd_z] for odd_z in range(2)] for odd_y in range(2)]

    def differences(field_y, field_z):
        along_y = [[None] * 2 for _ in range(2)]
        along_z = [[None] * 2 for _ in range(2)]
        for other in range(2):
            along_y[0][other] = field_y[1][other] - row_before(field_y[1][other])
            along_y[1][other] = row_after(field_y[0][other]) - field_y[0][other]
            along_z[other][0] = field_z[other][1] - lane_before(field_z[other][1])
            along_z[other][1] = lane_after(field_z[other][0]) - field_z[other][0]
        return along_y, along_z

    def store_flux(plane):
        there = in_grid(plane)
        ok = inside if there is None else inside & there
        here = density(plane)
        grad_y, grad_z = differences(here, here)
        flux_y = [[None] * 2 for _ in range(2)]
        flux_z = [[None] * 2 for _ in range(2)]
        by_density = [[None] * 2 for _ in range(2)]
        for odd_y in range(2):
            for odd_z in range(2):
                grad_x = dens[plane + 4, odd_y, odd_z] - dens[plane + 2, odd_y, odd_z]
                gy, gz = grad_y[odd_y][odd_z], grad_z[odd_y][odd_z]
                squared = grad_x * grad_x + gy * gy + gz * gz
                cells = jnp.where(ok, here[odd_y][odd_z], 1.0)
                inverse_root = jnp.exp(jnp.log(cells) * (-1.0 / 3.0))
                power_2 = inverse_root * inverse_root
                power_4 = power_2 * power_2
                inverse = 1.0 / (1.0 + DAMP * squared * (power_4 * power_4))
                by_density[odd_y][odd_z] = cells * power_2 * (B0 + inverse * (B1 + B2 * inverse))
                weight = jnp.where(ok, FLUX * power_4 * (inverse * inverse), 0.0)
                flux_x[plane + 2, odd_y, odd_z] = weight * grad_x
                flux_y[odd_y][odd_z] = weight * gy
                flux_z[odd_y][odd_z] = weight * gz
        if -1 <= plane <= FX:
            spread_y, spread_z = differences(flux_y, flux_z)
            for odd_y in range(2):
                for odd_z in range(2):
                    value[plane + 1, odd_y, odd_z] = by_density[odd_y][odd_z] - (
                        spread_y[odd_y][odd_z] + spread_z[odd_y][odd_z]
                    )

    for plane in range(-2, FX + 2):
        store_flux(plane)

    def potential(plane, odd_y, odd_z):
        there = in_grid(plane)
        ok = inside if there is None else inside & there
        cells = value[plane + 1, odd_y, odd_z] - (
            flux_x[plane + 3, odd_y, odd_z] - flux_x[plane + 1, odd_y, odd_z]
        )
        return jnp.where(ok, cells, 0.0)

    for index in range(CX):
        depth = [None, None]
        for odd_z in range(2):
            rows = []
            for odd_y in range(2):
                low = potential(2 * index - 1, odd_y, odd_z) + potential(2 * index + 2, odd_y, odd_z)
                mid = potential(2 * index, odd_y, odd_z) + potential(2 * index + 1, odd_y, odd_z)
                rows.append(0.125 * low + 0.375 * mid)
            depth[odd_z] = 0.125 * (row_before(rows[1]) + row_after(rows[0])) + 0.375 * (rows[0] + rows[1])
        cells = 0.125 * (lane_before(depth[1]) + lane_after(depth[0])) + 0.375 * (depth[0] + depth[1])
        for copy in range(PARTS):
            out[copy, index] = cells[RIM : RIM + YB]


SMEM = pl.BlockSpec(memory_space=pltpu.SMEM)
VMEM = pl.BlockSpec(memory_space=pltpu.VMEM)
HBM = pl.BlockSpec(memory_space=pltpu.HBM)
ANY = pl.BlockSpec(memory_space=pl.ANY)
F32 = jnp.float32


def is_dims(x):
    return isinstance(x, tuple) and all(isinstance(n, int) for n in x)


def call(kernel, name, out, in_specs, scratch=()):
    shapes = jax.tree.map(lambda dims: jax.ShapeDtypeStruct(dims, F32), out, is_leaf=is_dims)
    return pl.pallas_call(
        kernel,
        out_shape=shapes,
        in_specs=in_specs,
        out_specs=jax.tree.map(lambda dims: VMEM, out, is_leaf=is_dims),
        scratch_shapes=list(scratch),
        compiler_params=pltpu.CompilerParams(vmem_limit_bytes=32 * 2**20),
        name=name,
    )


def body(partial_density, moments, shape_functions, sphere_offsets, owned_count):
    slabs = lax.axis_size("dom")
    core_pairs = [(i, i ^ 1) for i in range(slabs)]
    second = [(i, (i + 2) % slabs) for i in range(slabs)]
    chip_pairs = []
    for b in range(PARTS):
        for i in range(slabs):
            j = i + 1 if i % 2 else i - 1
            there = (b, j) if 0 <= j < slabs else (b ^ 1, i)
            chip_pairs.append((b * slabs + i, there[0] * slabs + there[1]))

    total = pltpu.VMEM((2, 41, 80, 128), F32)
    windows = call(
        windows_kernel,
        "windows",
        (PARTS, CX, WY, CZ),
        [HBM],
        [pltpu.VMEM((CX, PARTS * YB, CZ), F32), pltpu.SemaphoreType.DMA((3,))],
    )(partial_density)
    windows = lax.all_to_all(windows, "band", 0, 0)

    packed, tail = call(
        blocks_kernel,
        "blocks",
        ((SLOTS, BLOCK + 128), (SLOTS, TAIL)),
        [SMEM, SMEM, VMEM, HBM],
        [pltpu.VMEM((NL, SLOTS, BLOCK), jnp.bfloat16), pltpu.SemaphoreType.DMA((3,))],
    )(sphere_offsets, owned_count, moments.T, shape_functions.transpose(1, 0, 2))
    dots_core = lax.ppermute(packed, "dom", core_pairs)
    dots_second = lax.ppermute(tail, "dom", second)
    dots_chip = lax.ppermute(packed, ("band", "dom"), chip_pairs)

    own, send_core, send_chip = call(
        own_kernel, "own_window", ((CX, WY, CZ), (2, WY, CZ), (2, WY, CZ)), [VMEM]
    )(windows)
    dots = call(
        place_own_kernel,
        "place_own",
        (2, FX + 6, 32, CZ),
        [SMEM, SMEM, VMEM],
        [pltpu.VMEM((64 + SLOTS * SBX * SBY + 128, 128), F32), total],
    )(sphere_offsets, owned_count, packed)
    core = lax.ppermute(send_core, "dom", core_pairs)
    chip = lax.ppermute(send_chip, ("band", "dom"), chip_pairs)

    dots = call(
        place_kernel,
        "place_others",
        (FX + 6, 2, 2, WY, CZ),
        [VMEM] * 4,
        [
            pltpu.VMEM((64 + SLOTS * (SBX + 5) * SBY + 128, 128), F32),
            total,
            pltpu.SMEM((3, SLOTS, 128), F32),
            pltpu.SemaphoreType.DMA((3,)),
        ],
    )(dots, dots_core, dots_chip, dots_second)
    result = call(
        main_kernel,
        "potential_of",
        (PARTS, CX, YB, CZ),
        [VMEM] * 4,
        [
            pltpu.VMEM((FX + 6, 2, 2, WY, CZ), F32),
            pltpu.VMEM((FX + 4, 2, 2, WY, CZ), F32),
            pltpu.VMEM((FX + 2, 2, 2, WY, CZ), F32),
        ],
    )(own, core, chip, dots)
    gathered = lax.all_to_all(result, "band", 0, 0)
    return gathered.transpose(1, 0, 2, 3).reshape(CX, PARTS * YB, CZ)


def solution(mesh):
    return jax.shard_map(
        body,
        mesh=mesh,
        in_specs=(
            P("band", "dom", None, None),
            P(None, "dom"),
            P("dom", None, None),
            P(None, "dom"),
            P("dom"),
        ),
        out_specs=P("dom", None, None),
        check_vma=False,
    )
```

time: 55.6 us -> 42 us (0.76)
  local copies, waits for them, and re-layouts: 10.3 us -> 2.48 us
  waiting for transfers between devices: 5.69 us -> 0.28 us
  Pallas kernels: 2.83 us -> 6.81 us
  other arithmetic: 2.88 us -> 0 us
    ppermute x5, waiting for transfers between devices: 5.69 us -> 0.28 us  [the longest x1 0.27 us: body(): dots_second = lax.ppermute(tail, 'dom', second)]
    pallas_call x2 -> x6, Pallas kernels: 2.83 us -> 6.81 us  [the longest x1 2.18 us: body(): call(place_kernel, 'place_others', (FX + 6, 2, 2, WY, CZ), [VMEM] * 4, [p...]
    reshape x3 -> x0, local copies, waits for them, and re-layouts: 2.89 us -> none  [the longest x1 2.72 us: body(): jnp.concatenate([blocks, before[:, :size]])]
    unnamed x14 -> x8, local copies, waits for them, and re-layouts: 4.58 us -> 1.71 us
    reduce_sum x1 -> x0, other arithmetic: 1.03 us -> none  [body(): own = lax.all_to_all(windows, 'band', 0, 0).sum(0)]
    concatenate x3 -> x0, other arithmetic: 0.91 us -> none  [the longest x1 0.81 us: body(): jnp.concatenate([blocks, before[:, :size]])]
    slice x2 -> x0, local copies, waits for them, and re-layouts: 0.81 us -> none  [the longest x1 0.8 us: body(): sphere_offsets[0]]
    mul x1 -> x0, other arithmetic: 0.75 us -> none  [body(): moments * live.astype(jnp.bfloat16)[None, :]]
  transfers between devices with their start and end apart: 6 -> 6, of which waited for: 1 -> 1; matrix products, arithmetic and copies ran while one was open for 19% -> 0% of each run, Pallas kernels for 2% -> 11%
where the time goes in v2:
time: 42 us; the launch traced here: 41.9 us
  starting transfers between devices  17.5 us (42%)
  blocking collectives  14 us (33%)
  Pallas kernels  6.81 us (16%)
  local copies, waits for them, and re-layouts  2.48 us (6%)
  between operations  0.77 us (2%)
    all_to_all x1, blocking collectives, body(): gathered = lax.all_to_all(result, 'band', 0, 0)  14 us
    ppermute x1, starting transfers between devices, body(): dots_chip = lax.ppermute(packed, ('band', 'dom'), chip_pairs)  6.19 us
    ppermute x1, starting transfers between devices, body(): chip = lax.ppermute(send_chip, ('band', 'dom'), chip_pairs)  6.05 us
    all_to_all x1, starting transfers between devices, body(): windows = lax.all_to_all(windows, 'band', 0, 0)  5.12 us
    pallas_call x1, Pallas kernels, body(): call(place_kernel, 'place_others', (FX + 6, 2, 2, WY, CZ), [VMEM] * 4, [p...  2.18 us
    unnamed x8, local copies, waits for them, and re-layouts  1.71 us
    pallas_call x1, Pallas kernels, body(): call(place_own_kernel, 'place_own', (2, FX + 6, 32, CZ), [SMEM, SMEM, VME...  1.33 us
    pallas_call x1, Pallas kernels, body(): call(main_kernel, 'potential_of', (PARTS, CX, YB, CZ), [VMEM] * 4, [pltpu...  1.17 us
  transfers between devices with their start and end apart: 6, of which 1 were waited for; matrix products, arithmetic and copies ran while one was open for 0% of the time, Pallas kernels for 11%

profile of v2, /device:TPU:4, one launch (start us, length us, event | category | flops | bytes accessed | tf_op | source)
XLA Modules:
  0.0 41.9 jit_solution(2463038453353820287)
XLA Ops:
  0.0 0.0 copy-start
  0.0 0.0 copy-start.1
  0.0 1.0 %copy-done.1 = f32[1,6,96,128]{3,2,1,0:T(8,128)S(1)} copy-done((f32[1,6,96,128]{3,2,1,0:T(8,128)S(1)}, f32[1,6,96,128]{3,2,1,0:T(8,128)}, u32[]{:S(2)}) %copy-start.1) | copy-done | bytes 294936
  1.1 1.1 %windows.1 = f32[8,6,16,128]{3,2,1,0:T(8,128)} custom-call(f32[1,6,96,128]{3,2,1,0:T(8,128)S(1)} %copy-done.1), custom_call_target="tpu_custom_call" | custom-call | tf_op jit(solution)/shard_map/windows/pallas_call | solution.py:398
  2.2 5.1 %all-to-all-start = ((f32[8,6,16,128]{3,2,1,0:T(8,128)}), f32[8,6,16,128]{3,2,1,0:T(8,128)S(1)}, u32[]{:S(2)}, u32[]{:S(2)}) async-start(f32[8,6,16,128]{3,2,1,0:T(8,128)} %windows.1), calls=%async_computation | async-start | bytes 786432 | tf_op jit(solution)/shard_map/all_to_all | solution.py:405
  7.3 0.0 copy-start.3
  8.0 0.0 copy-start.2
  8.0 0.0 copy-done
  8.0 0.0 copy-done.3
  8.0 0.7 %copy-done.2 = s32[3,8]{1,0:T(4,128)S(1)} copy-done((s32[3,8]{1,0:T(4,128)S(1)}, s32[3,8]{1,0:T(4,128)}, u32[]{:S(2)}) %copy-start.2) | copy-done | bytes 120
  8.7 0.9 %blocks.1 = (f32[8,7040]{1,0:T(8,128)S(1)}, f32[8,1280]{1,0:T(8,128)S(1)}) custom-call(s32[3,8]{1,0:T(4,128)S(1)} %copy-done.2, s32[1]{0:T(128)S(6)} %copy.7.count, bf16[8,9]{1,0:T(8,128)(2,1)S(1)} %bitcast.4, bf16[9,8,6912]{2,1,0:T(8,128)(2,1)S(1)} %bitcast.3), custom_call_target="tpu_custom_call" | custom-call | tf_op jit(solution)/shard_map/blocks/pallas_call | solution.py:407
  9.6 0.1 collective-permute-start.2
  9.7 6.2 %collective-permute-start.3 = (f32[8,7040]{1,0:T(8,128)S(1)}, f32[8,7040]{1,0:T(8,128)S(1)}, u32[]{:S(2)}, u32[]{:S(2)}) collective-permute-start(f32[8,7040]{1,0:T(8,128)S(1)} %get-tuple-element.13.own), channel_id=1, source_target_pairs={{0,32},{1,2},{2,1},{3,4},{4,3},{5,6},{6,5},{7,8},{8,7},{9,10},{10,... | collective-permute-start | bytes 675848 | tf_op jit(solution)/shard_map/ppermute | solution.py:416
  15.9 0.0 collective-permute-start.4
  15.9 0.0 all-to-all-done.windows
  16.0 0.1 collective-permute-start
  16.1 6.0 %collective-permute-start.1 = (f32[2,16,128]{2,1,0:T(8,128)S(1)}, f32[2,16,128]{2,1,0:T(8,128)S(1)}, u32[]{:S(2)}, u32[]{:S(2)}) collective-permute-start(f32[2,16,128]{2,1,0:T(8,128)S(1)} %get-tuple-element.12), channel_id=1, source_target_pairs={{0,32},{1,2},{2,1},{3,4},{4,3},{5,6},{6,5},{7,8},{8,7},{9,10},{10,... | collective-permute-start | bytes 49160 | tf_op jit(solution)/shard_map/ppermute | solution.py:429
  22.1 1.3 %place_own.1.own = f32[2,18,32,128]{3,2,1,0:T(8,128)S(1)} custom-call(s32[3,8]{1,0:T(4,128)S(1)} %copy-done.2, s32[1]{0:T(128)S(6)} %copy.7.count, f32[8,7040]{1,0:T(8,128)S(1)} %get-tuple-element.13.own), custom_call_target="tpu_custom_call" | custom-call | tf_op jit(solution)/shard_map/place_own/pallas_call | solution.py:421
  23.5 0.3 collective-permute-done.4.second
  23.7 0.0 collective-permute-done.2.core
  23.7 0.0 collective-permute-done.3.chip
  23.7 2.2 %place_others.1.dots = f32[18,2,2,16,128]{4,3,2,1,0:T(8,128)S(1)} custom-call(f32[2,18,32,128]{3,2,1,0:T(8,128)S(1)} %place_own.1.own, f32[8,7040]{1,0:T(8,128)S(1)} %collective-permute-done.2.core, f32[8,7040]{1,0:T(8,128)S(1)} %collective-permute-done.3.chip, f32[8,1280]{1,0:T(8,128)S(1)} %collective-permute-done.4.second), custom_call_target="tpu_custom_call" | custom-call | tf_op jit(solution)/shard_map/place_others/pallas_call | solution.py:431
  25.9 0.0 collective-permute-done.core
  25.9 0.0 collective-permute-done.1.chip
  25.9 1.2 %potential_of.1 = f32[8,6,12,128]{3,2,1,0:T(8,128)S(1)} custom-call(f32[6,16,128]{2,1,0:T(8,128)S(1)} %get-tuple-element.10.own, f32[2,16,128]{2,1,0:T(8,128)S(1)} %collective-permute-done.core, f32[2,16,128]{2,1,0:T(8,128)S(1)} %collective-permute-done.1.chip, f32[18,2,2,16,128]{4,3,2,1,0:T(8,128)S(1)} %place_others.1.dots), custom_call_target="tpu_custom_call" | custom-call | tf_op jit(solution)/shard_map/potential_of/pallas_call | solution.py:443
  27.1 14.0 %all_to_all.10 = f32[8,6,12,128]{3,2,1,0:T(8,128)S(1)} all-to-all(f32[8,6,12,128]{3,2,1,0:T(8,128)S(1)} %potential_of.1), channel_id=1, replica_groups=mesh['band'=8,'dom'=32] {'band'}, dimensions={0} | all-to-all | bytes 589824 | tf_op jit(solution)/shard_map/all_to_all | solution.py:454
  41.2 0.7 %reshape.3 = f32[6,96,128]{2,1,0:T(8,128)} reshape(f32[6,8,12,128]{3,2,1,0:T(8,128)S(1)} %copy.6) | data formatting | bytes 589824 | tf_op jit(solution)/shard_map/reshape | solution.py:455
  (2 shorter events, 0.1 us)
Async XLA Ops:
  0.0 8.0 %copy-start = (bf16[8,9,6912]{2,0,1:T(8,128)(2,1)S(1)}, bf16[8,9,6912]{2,0,1:T(8,128)(2,1)}, u32[]{:S(2)}) copy-start(bf16[8,9,6912]{2,0,1:T(8,128)(2,1)} %param.7) | copy-start | bytes 2985988
  0.0 1.0 %copy-start.1 = (f32[1,6,96,128]{3,2,1,0:T(8,128)S(1)}, f32[1,6,96,128]{3,2,1,0:T(8,128)}, u32[]{:S(2)}) copy-start(f32[1,6,96,128]{3,2,1,0:T(8,128)} %cells.1) | copy-start | bytes 884740
  2.2 13.7 %all-to-all-start = ((f32[8,6,16,128]{3,2,1,0:T(8,128)}), f32[8,6,16,128]{3,2,1,0:T(8,128)S(1)}, u32[]{:S(2)}, u32[]{:S(2)}) async-start(f32[8,6,16,128]{3,2,1,0:T(8,128)} %windows.1), calls=%async_computation | async-start | bytes 786432 | tf_op jit(solution)/shard_map/all_to_all | solution.py:405
  7.3 0.7 %copy-start.3 = (bf16[9,8]{0,1:T(8,128)(2,1)S(1)}, bf16[9,8]{0,1:T(8,128)(2,1)}, u32[]{:S(2)}) copy-start(bf16[9,8]{0,1:T(8,128)(2,1)} %param.6) | copy-start | bytes 436
  8.0 0.7 %copy-start.2 = (s32[3,8]{1,0:T(4,128)S(1)}, s32[3,8]{1,0:T(4,128)}, u32[]{:S(2)}) copy-start(s32[3,8]{1,0:T(4,128)} %offsets.3) | copy-start | bytes 292
  9.6 14.1 %collective-permute-start.2 = (f32[8,7040]{1,0:T(8,128)S(1)}, f32[8,7040]{1,0:T(8,128)S(1)}, u32[]{:S(2)}, u32[]{:S(2)}) collective-permute-start(f32[8,7040]{1,0:T(8,128)S(1)} %get-tuple-element.13.own), channel_id=1, source_target_pairs={{0,1},{1,0},{2,3},{3,2},{4,5},{5,4},{6,7},{7,6},{8,9},{9,8},{10,11... | collective-permute-start | bytes 675848 | tf_op jit(solution)/shard_map/ppermute | solution.py:414
  9.7 14.0 %collective-permute-start.3 = (f32[8,7040]{1,0:T(8,128)S(1)}, f32[8,7040]{1,0:T(8,128)S(1)}, u32[]{:S(2)}, u32[]{:S(2)}) collective-permute-start(f32[8,7040]{1,0:T(8,128)S(1)} %get-tuple-element.13.own), channel_id=1, source_target_pairs={{0,32},{1,2},{2,1},{3,4},{4,3},{5,6},{6,5},{7,8},{8,7},{9,10},{10,... | collective-permute-start | bytes 675848 | tf_op jit(solution)/shard_map/ppermute | solution.py:416
  15.9 7.8 %collective-permute-start.4 = (f32[8,1280]{1,0:T(8,128)S(1)}, f32[8,1280]{1,0:T(8,128)S(1)}, u32[]{:S(2)}, u32[]{:S(2)}) collective-permute-start(f32[8,1280]{1,0:T(8,128)S(1)} %get-tuple-element.14), channel_id=1, source_target_pairs={{0,2},{1,3},{2,4},{3,5},{4,6},{5,7},{6,8},{7,9},{8,10},{9,11},{10,... | collective-permute-start | bytes 122888 | tf_op jit(solution)/shard_map/ppermute | solution.py:415
  16.0 10.0 %collective-permute-start = (f32[2,16,128]{2,1,0:T(8,128)S(1)}, f32[2,16,128]{2,1,0:T(8,128)S(1)}, u32[]{:S(2)}, u32[]{:S(2)}) collective-permute-start(f32[2,16,128]{2,1,0:T(8,128)S(1)} %get-tuple-element.11), channel_id=1, source_target_pairs={{0,1},{1,0},{2,3},{3,2},{4,5},{5,4},{6,7},{7,6},{8,9},{9,8},{10,11... | collective-permute-start | bytes 49160 | tf_op jit(solution)/shard_map/ppermute | solution.py:428
  16.1 9.9 %collective-permute-start.1 = (f32[2,16,128]{2,1,0:T(8,128)S(1)}, f32[2,16,128]{2,1,0:T(8,128)S(1)}, u32[]{:S(2)}, u32[]{:S(2)}) collective-permute-start(f32[2,16,128]{2,1,0:T(8,128)S(1)} %get-tuple-element.12), channel_id=1, source_target_pairs={{0,32},{1,2},{2,1},{3,4},{4,3},{5,6},{6,5},{7,8},{8,7},{9,10},{10,... | collective-permute-start | bytes 49160 | tf_op jit(solution)/shard_map/ppermute | solution.py:429

commit v3 on v2

--- a/solution.py
+++ b/solution.py
@@ -33,92 +33,85 @@
 FLUX = 2.0 * HALF_INVERSE**2 * PREFACTOR * MU / SCALE
 
 
-def windows_kernel(cells, windows, held, sems):
-    copies = []
-    for third in range(3):
-        planes = pl.ds(2 * third, 2)
-        copies.append(pltpu.make_async_copy(cells.at[0, planes], held.at[planes], sems.at[third]))
-        copies[-1].start()
-    for third in range(3):
-        copies[third].wait()
-        planes = pl.ds(2 * third, 2)
-        for part in range(PARTS):
-            first = YB * part - RIM
-            low, high = max(first, 0), min(first + WY, PARTS * YB)
-            rows = held[planes, low:high, :]
-            if low > first:
-                rows = jnp.concatenate([jnp.zeros((2, low - first, CZ), jnp.float32), rows], axis=1)
-            if high < first + WY:
-                rows = jnp.concatenate([rows, jnp.zeros((2, first + WY - high, CZ), jnp.float32)], axis=1)
-            windows[part, planes] = rows
-
-
-def blocks_kernel(offsets, count, moments, shapes, packed, tail, held, sems):
-    step = BLOCK // 3
-    copies = []
-    for third in range(3):
-        lanes = pl.ds(step * third, step)
-        copies.append(
-            pltpu.make_async_copy(shapes.at[:, :, lanes], held.at[:, :, lanes], sems.at[third])
-        )
-        copies[-1].start()
-    row = lax.broadcasted_iota(jnp.int32, (SLOTS, 128), 0)
+def windows_kernel(cells, windows):
+    for part in range(PARTS):
+        first = YB * part - RIM
+        low, high = max(first, 0), min(first + WY, PARTS * YB)
+        rows = cells[0, :, low:high, :]
+        if low > first:
+            rows = jnp.concatenate([jnp.zeros((CX, low - first, CZ), jnp.float32), rows], axis=1)
+        if high < first + WY:
+            rows = jnp.concatenate([rows, jnp.zeros((CX, first + WY - high, CZ), jnp.float32)], axis=1)
+        windows[part] = rows
+
+
+def blocks_kernel(offsets, count, moments, shapes, packed, tail):
+    row = lax.broadcasted_iota(jnp.int32, (SLOTS, SLOTS), 0)
+    lane = lax.broadcasted_iota(jnp.int32, (SLOTS, SLOTS), 1)
+    slot = lax.broadcasted_iota(jnp.int32, (SLOTS, 1), 0)
+    alive = slot < count[...]
+    where = lax.broadcasted_iota(jnp.int32, (SLOTS, 128), 1)
+    info = jnp.zeros((SLOTS, 128), jnp.float32)
+    for dim in range(3):
+        values = jnp.broadcast_to(offsets[dim : dim + 1, :], (SLOTS, SLOTS)).astype(jnp.float32)
+        column = jnp.sum(jnp.where(row == lane, values, 0.0), axis=1, keepdims=True)
+        if dim == 1:
+            column = jnp.where(alive, column, float(FAR))
+        info = jnp.where(where == dim, column, info)
+    packed[:, BLOCK : BLOCK + 128] = info
+    weights = jnp.where(alive, moments[...].astype(jnp.float32), 0.0)
+    step = BLOCK // 9
+    for chunk in range(9):
+        lanes = pl.ds(chunk * step, step)
+        total = weights[:, 0:1] * shapes[0, :, lanes].astype(jnp.float32)
+        for channel in range(1, NL):
+            total = total + weights[:, channel : channel + 1] * shapes[channel, :, lanes].astype(
+                jnp.float32
+            )
+        packed[:, lanes] = total
+    tail[...] = packed[:, BLOCK + 128 - TAIL :]
+
+
+def line_up(read, depth_x, begin, flat):
     lane = lax.broadcasted_iota(jnp.int32, (SLOTS, 128), 1)
-    info = jnp.zeros((SLOTS, 128), jnp.int32)
-    for which in range(SLOTS):
-        for dim in range(3):
-            value = offsets[dim, which]
-            if dim == 1:
-                value = jnp.where(which < count[0], value, FAR)
-            info = jnp.where((row == which) & (lane == dim), value, info)
-    packed[:, BLOCK : BLOCK + 128] = info.astype(jnp.float32)
-    slot = lax.broadcasted_iota(jnp.int32, (SLOTS, 1), 0)
-    weights = jnp.where(slot < count[0], moments[...].astype(jnp.float32), 0.0)
-    for third in range(3):
-        copies[third].wait()
-        for chunk in range(3):
-            lanes = pl.ds(step * third + chunk * (step // 3), step // 3)
-            total = weights[:, 0:1] * held[0, :, lanes].astype(jnp.float32)
-            for channel in range(1, NL):
-                total = total + weights[:, channel : channel + 1] * held[channel, :, lanes].astype(
-                    jnp.float32
-                )
-            packed[:, lanes] = total
-    tail[...] = packed[:, BLOCK + 128 - TAIL :]
-
-
-def spread_blocks(sources, flat, total):
+    tiles = {}
+    for line in range(depth_x * SBY):
+        tile, skip = divmod(line * SBZ, 128)
+        for needed in (tile, tile + 1) if skip + SBZ > 128 else (tile,):
+            if needed not in tiles:
+                tiles = {k: v for k, v in tiles.items() if k >= tile}
+                tiles[needed] = read(needed)
+        cells = tiles[tile]
+        if skip + SBZ > 128:
+            cells = jnp.where(lane >= skip, cells, tiles[tile + 1])
+        if skip:
+            cells = pltpu.roll(cells, 128 - skip, 1)
+        flat[pl.ds(64 + SLOTS * (begin * SBY + line), SLOTS), :] = jnp.where(lane < SBZ, cells, 0.0)
+
+
+def whole_offsets(offsets, counts):
     lane = lax.broadcasted_iota(jnp.int32, (SLOTS, 128), 1)
-    for read, depth_x, _, begin, _, _ in sources:
-        tiles = {}
-        for line in range(depth_x * SBY):
-            tile, skip = divmod(line * SBZ, 128)
-            for needed in (tile, tile + 1) if skip + SBZ > 128 else (tile,):
-                if needed not in tiles:
-                    tiles = {k: v for k, v in tiles.items() if k >= tile}
-                    tiles[needed] = read(needed)
-            cells = tiles[tile]
-            if skip + SBZ > 128:
-                cells = jnp.where(lane >= skip, cells, tiles[tile + 1])
-            if skip:
-                cells = pltpu.roll(cells, 128 - skip, 1)
-            flat[pl.ds(64 + SLOTS * (begin * SBY + line), SLOTS), :] = jnp.where(lane < SBZ, cells, 0.0)
-    column = lax.broadcasted_iota(jnp.int32, (128, 256), 1)
-    fine_z = jnp.where(column < 128, 2 * column, 2 * column - 255)
-    inner_z = fine_z - lax.broadcasted_iota(jnp.int32, (128, 256), 0)
-    row_z = lax.broadcasted_iota(jnp.int32, (128, 256), 0) < SBZ
+    whole = offsets.astype(jnp.int32)
+    row = jnp.max(jnp.where(lane == 0, whole, 0), axis=1, keepdims=True)
+    there = whole - 2 * (YB * lax.axis_index("band") - RIM) + 24
+    return jnp.where(lane == 1, jnp.where(counts(row), there, FAR), whole)
+
+
+def spread_blocks(sources, flat, total, info):
+    column = lax.broadcasted_iota(jnp.int32, (256, 256), 1)
+    line = lax.rem(lax.broadcasted_iota(jnp.int32, (256, 256), 0), 128)
+    inner_z = jnp.where(column < 128, 2 * column, 2 * column - 255) - line
+    inner_z = jnp.where(line < SBZ, inner_z, -1)
     row_y = lax.broadcasted_iota(jnp.int32, (32, 128), 0)
-    first_row = 2 * (YB * lax.axis_index("band") - RIM)
-    for _, depth_x, first_plane, begin, value, there in sources:
+    for which, (depth_x, first_plane, begin) in enumerate(sources):
 
         def one(slot, carry):
-            row = value(slot, 0)
-            col = value(slot, 1) - first_row + 24
-            depth = value(slot, 2)
-            meets = (col > 0) & (col < 56)
-
-            @pl.when(meets if there is None else meets & there)
+            col = info[which, slot, 1]
+
+            @pl.when((col > 0) & (col < 56))
             def _():
+                row = info[which, slot, 0]
+                depth = info[which, slot, 2]
                 shift = lax.rem(col, 8)
                 base = pl.multiple_of(col - shift, 8)
                 held = (row_y >= shift) & (row_y < shift + SBY)
@@ -129,9 +122,9 @@
                 block = jnp.concatenate(parts, axis=0)
                 high = block.astype(jnp.bfloat16)
                 low = (block - high.astype(jnp.float32)).astype(jnp.bfloat16)
-                pick = jnp.where((inner_z == depth) & row_z, 1.0, 0.0).astype(jnp.bfloat16)
-                spread = jnp.dot(high, pick, preferred_element_type=jnp.float32)
-                spread = spread + jnp.dot(low, pick, preferred_element_type=jnp.float32)
+                pick = jnp.where(inner_z == depth, 1.0, 0.0).astype(jnp.bfloat16)
+                both = jnp.concatenate([high, low], axis=1)
+                spread = jnp.dot(both, pick, preferred_element_type=jnp.float32)
                 planes = pl.ds(row + first_plane, depth_x)
                 rows = pl.ds(base, 32)
                 spread = spread.reshape(depth_x, 32, 256)
@@ -144,36 +137,23 @@
         lax.fori_loop(0, SLOTS, one, 0)
 
 
-def place_own_kernel(offsets, count, own, out, flat, total):
+def place_kernel(own, core, chip, out, flat, total, whole, info, sem):
+    slab = lax.axis_index("dom")
+    even_slab = lax.rem(slab, 2) == 0
+    last = lax.axis_size("dom") - 1
+    lanes = pl.ds(BLOCK, 128)
+    before = jnp.where(even_slab, chip[:, lanes], core[:, lanes])
+    after = jnp.where(even_slab, core[:, lanes], chip[:, lanes])
+    whole[0] = whole_offsets(own[:, lanes], lambda row: row >= 0)
+    whole[1] = whole_offsets(before, lambda row: (row >= 0) & (slab > 0))
+    whole[2] = whole_offsets(after, lambda row: (row < 3) & (slab < last))
+    copy = pltpu.make_async_copy(whole, info, sem)
+    copy.start()
     for odd_z in range(2):
         total[odd_z, pl.ds(11, 18), pl.ds(24, 32), :] = jnp.zeros((18, 32, 128), jnp.float32)
 
-    def read(tile):
+    def own_tile(tile):
         return own[:, 128 * tile : 128 * tile + 128]
-
-    def value(slot, which):
-        if which == 1:
-            return jnp.where(slot < count[0], offsets[1, slot], FAR)
-        return offsets[which, slot]
-
-    spread_blocks([(read, SBX, 14, 0, value, None)], flat, total)
-    for odd_z in range(2):
-        out[odd_z] = total[odd_z, pl.ds(11, 18), pl.ds(24, 32), :]
-
-
-def place_kernel(own, core, chip, second, out, flat, total, info, sems):
-    slab = lax.axis_index("dom")
-    even_slab = lax.rem(slab, 2) == 0
-    copies = []
-    for index, (ref, start) in enumerate(
-        ((core, BLOCK), (chip, BLOCK), (second, TAIL - 128))
-    ):
-        copies.append(
-            pltpu.make_async_copy(ref.at[:, pl.ds(start, 128)], info.at[index], sems.at[index])
-        )
-        copies[-1].start()
-    for odd_z in range(2):
-        total[odd_z, pl.ds(11, 18), pl.ds(24, 32), :] = own[odd_z]
 
     def before_tile(tile):
         lanes = pl.ds(128 * tile, 128)
@@ -183,28 +163,11 @@
         lanes = pl.ds(128 * tile, 128)
         return jnp.where(even_slab, core[:, lanes], chip[:, lanes])
 
-    def second_tile(tile):
-        return second[:, 128 * tile : 128 * tile + 128]
-
-    def value_of(if_even, if_odd):
-        def value(slot, which):
-            both = jnp.where(even_slab, info[if_even, slot, which], info[if_odd, slot, which])
-            return both.astype(jnp.int32)
-
-        return value
-
-    for copy in copies:
-        copy.wait()
-    last = lax.axis_size("dom") - 1
-    spread_blocks(
-        [
-            (before_tile, SBX, 2, 0, value_of(1, 0), slab > 0),
-            (after_tile, 3, 26, SBX, value_of(0, 1), slab < last),
-            (second_tile, 2, 0, SBX + 3, value_of(2, 2), slab > 1),
-        ],
-        flat,
-        total,
-    )
+    line_up(own_tile, SBX, 0, flat)
+    line_up(before_tile, SBX, SBX, flat)
+    line_up(after_tile, 3, 2 * SBX, flat)
+    copy.wait()
+    spread_blocks([(SBX, 14, 0), (SBX, 2, SBX), (3, 26, 2 * SBX)], flat, total, info)
     for plane in range(FX + 6):
         for odd_y in range(2):
             for odd_z in range(2):
@@ -220,14 +183,21 @@
         own[plane] = cells
     even_slab = lax.rem(lax.axis_index("dom"), 2) == 0
     send_core[...] = jnp.where(even_slab, own[CX - 2 : CX], own[0:2])
-    send_chip[...] = jnp.where(even_slab, own[0:2], own[CX - 2 : CX])
-
-
-def main_kernel(own, core, chip, dots, out, dens, flux_x, value):
+    send_chip[0:2] = jnp.where(even_slab, own[0:2], own[CX - 2 : CX])
+    send_chip[2:4] = own[2:4]
+
+
+def main_kernel(own, core, chip, dots, second, out, dens, flux_x, value, flat, total, whole, info, sem):
     slab = lax.axis_index("dom")
     part = lax.axis_index("band")
     last = lax.axis_size("dom") - 1
     even_slab = lax.rem(slab, 2) == 0
+    whole[0] = whole_offsets(second[:, pl.ds(TAIL - 128, 128)], lambda row: (row >= 10) & (slab > 1))
+    copy = pltpu.make_async_copy(whole, info, sem)
+    copy.start()
+    for odd_z in range(2):
+        total[odd_z, pl.ds(0, 4), pl.ds(24, 32), :] = jnp.zeros((4, 32, CZ), jnp.float32)
+    line_up(lambda tile: second[:, 128 * tile : 128 * tile + 128], 2, 0, flat)
     lane = lax.broadcasted_iota(jnp.int32, (WY, CZ), 1)
     first_lane = lane == 0
     last_lane = lane == CZ - 1
@@ -272,6 +242,9 @@
         if plane >= FX:
             return slab < last
         return None
+
+    copy.wait()
+    spread_blocks([(2, -10, 0)], flat, total, info)
 
     grids = {}
     for plane in range(-3, FX + 3):
@@ -288,6 +261,8 @@
             for odd_z in range(2):
                 cells = 0.75 * grids[index][odd_y][odd_z] + 0.25 * grids[near][odd_y][odd_z]
                 cells = cells + dots[plane + 3, odd_y, odd_z]
+                if plane < -1:
+                    cells = cells + total[odd_z, plane + 4, pl.ds(24 + odd_y, WY, stride=2), :]
                 dens[plane + 3, odd_y, odd_z] = jnp.where(ok, cells, 0.0)
 
     def density(plane):
@@ -361,8 +336,6 @@
 
 SMEM = pl.BlockSpec(memory_space=pltpu.SMEM)
 VMEM = pl.BlockSpec(memory_space=pltpu.VMEM)
-HBM = pl.BlockSpec(memory_space=pltpu.HBM)
-ANY = pl.BlockSpec(memory_space=pl.ANY)
 F32 = jnp.float32
 
 
@@ -394,63 +367,53 @@
             there = (b, j) if 0 <= j < slabs else (b ^ 1, i)
             chip_pairs.append((b * slabs + i, there[0] * slabs + there[1]))
 
-    total = pltpu.VMEM((2, 41, 80, 128), F32)
-    windows = call(
-        windows_kernel,
-        "windows",
-        (PARTS, CX, WY, CZ),
-        [HBM],
-        [pltpu.VMEM((CX, PARTS * YB, CZ), F32), pltpu.SemaphoreType.DMA((3,))],
-    )(partial_density)
+    windows = call(windows_kernel, "windows", (PARTS, CX, WY, CZ), [VMEM])(partial_density)
     windows = lax.all_to_all(windows, "band", 0, 0)
 
     packed, tail = call(
         blocks_kernel,
         "blocks",
         ((SLOTS, BLOCK + 128), (SLOTS, TAIL)),
-        [SMEM, SMEM, VMEM, HBM],
-        [pltpu.VMEM((NL, SLOTS, BLOCK), jnp.bfloat16), pltpu.SemaphoreType.DMA((3,))],
-    )(sphere_offsets, owned_count, moments.T, shape_functions.transpose(1, 0, 2))
+        [VMEM] * 4,
+    )(sphere_offsets, owned_count.reshape(1, 1), moments.T, shape_functions.transpose(1, 0, 2))
     dots_core = lax.ppermute(packed, "dom", core_pairs)
     dots_second = lax.ppermute(tail, "dom", second)
     dots_chip = lax.ppermute(packed, ("band", "dom"), chip_pairs)
 
     own, send_core, send_chip = call(
-        own_kernel, "own_window", ((CX, WY, CZ), (2, WY, CZ), (2, WY, CZ)), [VMEM]
+        own_kernel, "own_window", ((CX, WY, CZ), (2, WY, CZ), (4, WY, CZ)), [VMEM]
     )(windows)
-    dots = call(
-        place_own_kernel,
-        "place_own",
-        (2, FX + 6, 32, CZ),
-        [SMEM, SMEM, VMEM],
-        [pltpu.VMEM((64 + SLOTS * SBX * SBY + 128, 128), F32), total],
-    )(sphere_offsets, owned_count, packed)
     core = lax.ppermute(send_core, "dom", core_pairs)
     chip = lax.ppermute(send_chip, ("band", "dom"), chip_pairs)
-
     dots = call(
         place_kernel,
-        "place_others",
+        "place_spheres",
         (FX + 6, 2, 2, WY, CZ),
-        [VMEM] * 4,
+        [VMEM] * 3,
         [
-            pltpu.VMEM((64 + SLOTS * (SBX + 5) * SBY + 128, 128), F32),
-            total,
-            pltpu.SMEM((3, SLOTS, 128), F32),
-            pltpu.SemaphoreType.DMA((3,)),
+            pltpu.VMEM((64 + SLOTS * (2 * SBX + 3) * SBY + 128, 128), F32),
+            pltpu.VMEM((2, 41, 80, CZ), F32),
+            pltpu.VMEM((3, SLOTS, 128), jnp.int32),
+            pltpu.SMEM((3, SLOTS, 128), jnp.int32),
+            pltpu.SemaphoreType.DMA,
         ],
-    )(dots, dots_core, dots_chip, dots_second)
+    )(packed, dots_core, dots_chip)
     result = call(
         main_kernel,
         "potential_of",
         (PARTS, CX, YB, CZ),
-        [VMEM] * 4,
+        [VMEM] * 5,
         [
             pltpu.VMEM((FX + 6, 2, 2, WY, CZ), F32),
             pltpu.VMEM((FX + 4, 2, 2, WY, CZ), F32),
             pltpu.VMEM((FX + 2, 2, 2, WY, CZ), F32),
+            pltpu.VMEM((64 + SLOTS * 2 * SBY + 128, 128), F32),
+            pltpu.VMEM((2, 4, 80, CZ), F32),
+            pltpu.VMEM((1, SLOTS, 128), jnp.int32),
+            pltpu.SMEM((1, SLOTS, 128), jnp.int32),
+            pltpu.SemaphoreType.DMA,
         ],
-    )(own, core, chip, dots)
+    )(own, core, chip, dots, dots_second)
     gathered = lax.all_to_all(result, "band", 0, 0)
     return gathered.transpose(1, 0, 2, 3).reshape(CX, PARTS * YB, CZ)
 

time: 42 us -> 39.7 us (0.945)
  starting transfers between devices: 17.5 us -> 15.1 us
  waiting for transfers between devices: 0.28 us -> 2.01 us
  Pallas kernels: 6.81 us -> 5.5 us
    ppermute x1, starting transfers between devices: 6.05 us -> 3.68 us  [body(): chip = lax.ppermute(send_chip, ('band', 'dom'), chip_pairs)]
    pallas_call x6 -> x5, Pallas kernels: 6.81 us -> 5.5 us  [the longest x1 2.22 us: body(): call(place_kernel, 'place_spheres', (FX + 6, 2, 2, WY, CZ), [VMEM] * 3, [...]
    ppermute x1, waiting for transfers between devices: 0.27 us -> 1.56 us  [body(): dots_second = lax.ppermute(tail, 'dom', second)]
    all_to_all x1, waiting for transfers between devices: 0.01 us -> 0.44 us  [body(): windows = lax.all_to_all(windows, 'band', 0, 0)]
  transfers between devices with their start and end apart: 6 -> 6, of which waited for: 1 -> 2; matrix products, arithmetic and copies ran while one was open for 0% -> 0% of each run, Pallas kernels for 11% -> 7%
where the time goes in v3:
time: 39.7 us; the launch traced here: 39.5 us
  starting transfers between devices  15.1 us (38%)
  blocking collectives  13.8 us (35%)
  Pallas kernels  5.5 us (14%)
  local copies, waits for them, and re-layouts  2.41 us (6%)
  waiting for transfers between devices  2.01 us (5%)
  between operations  0.73 us (2%)
    all_to_all x1, blocking collectives, body(): gathered = lax.all_to_all(result, 'band', 0, 0)  13.8 us
    ppermute x1, starting transfers between devices, body(): dots_chip = lax.ppermute(packed, ('band', 'dom'), chip_pairs)  6.19 us
    all_to_all x1, starting transfers between devices, body(): windows = lax.all_to_all(windows, 'band', 0, 0)  5.1 us
    ppermute x1, starting transfers between devices, body(): chip = lax.ppermute(send_chip, ('band', 'dom'), chip_pairs)  3.68 us
    pallas_call x1, Pallas kernels, body(): call(place_kernel, 'place_spheres', (FX + 6, 2, 2, WY, CZ), [VMEM] * 3, [...  2.22 us
    pallas_call x1, Pallas kernels, body(): call(main_kernel, 'potential_of', (PARTS, CX, YB, CZ), [VMEM] * 5, [pltpu...  2.12 us
    unnamed x8, local copies, waits for them, and re-layouts  1.64 us
    ppermute x1, waiting for transfers between devices, body(): dots_second = lax.ppermute(tail, 'dom', second)  1.56 us
  transfers between devices with their start and end apart: 6, of which 2 were waited for; matrix products, arithmetic and copies ran while one was open for 0% of the time, Pallas kernels for 7%

profile of v3, /device:TPU:4, one launch (start us, length us, event | category | flops | bytes accessed | tf_op | source)
XLA Modules:
  0.0 39.5 jit_solution(7818364324766602071)
XLA Ops:
  0.0 0.0 copy-start.1
  0.0 1.0 %copy-done.1 = f32[1,6,96,128]{3,2,1,0:T(8,128)S(1)} copy-done((f32[1,6,96,128]{3,2,1,0:T(8,128)S(1)}, f32[1,6,96,128]{3,2,1,0:T(8,128)}, u32[]{:S(2)}) %copy-start.1) | copy-done | bytes 294936
  1.0 0.0 copy-start
  1.0 0.8 %windows.1 = f32[8,6,16,128]{3,2,1,0:T(8,128)} custom-call(f32[1,6,96,128]{3,2,1,0:T(8,128)S(1)} %copy-done.1), custom_call_target="tpu_custom_call" | custom-call | tf_op jit(solution)/shard_map/windows/pallas_call | solution.py:370
  1.7 5.1 %all-to-all-start = ((f32[8,6,16,128]{3,2,1,0:T(8,128)}), f32[8,6,16,128]{3,2,1,0:T(8,128)S(1)}, u32[]{:S(2)}, u32[]{:S(2)}) async-start(f32[8,6,16,128]{3,2,1,0:T(8,128)} %windows.1), calls=%async_computation | async-start | bytes 786432 | tf_op jit(solution)/shard_map/all_to_all | solution.py:371
  7.5 0.0 copy-start.3
  7.5 0.0 copy-start.2
  7.5 0.0 copy-done
  7.5 0.7 %copy-done.3 = bf16[9,8]{0,1:T(8,128)(2,1)S(1)} copy-done((bf16[9,8]{0,1:T(8,128)(2,1)S(1)}, bf16[9,8]{0,1:T(8,128)(2,1)}, u32[]{:S(2)}) %copy-start.3) | copy-done | bytes 168
  8.2 0.0 copy-done.2
  8.2 0.4 blocks.1
  8.6 0.1 collective-permute-start.2
  8.7 6.2 %collective-permute-start.3 = (f32[8,7040]{1,0:T(8,128)S(1)}, f32[8,7040]{1,0:T(8,128)S(1)}, u32[]{:S(2)}, u32[]{:S(2)}) collective-permute-start(f32[8,7040]{1,0:T(8,128)S(1)} %get-tuple-element.13.own), channel_id=1, source_target_pairs={{0,32},{1,2},{2,1},{3,4},{4,3},{5,6},{6,5},{7,8},{8,7},{9,10},{10,... | collective-permute-start | bytes 675848 | tf_op jit(solution)/shard_map/ppermute | solution.py:381
  14.9 0.0 collective-permute-start.4
  14.9 0.4 %all-to-all-done.windows = f32[8,6,16,128]{3,2,1,0:T(8,128)S(1)} async-done(((f32[8,6,16,128]{3,2,1,0:T(8,128)}), f32[8,6,16,128]{3,2,1,0:T(8,128)S(1)}, u32[]{:S(2)}, u32[]{:S(2)}) %all-to-all-start) | async-done | bytes 393248 | tf_op jit(solution)/shard_map/all_to_all | solution.py:371
  15.3 3.7 %collective-permute-start.1 = (f32[4,16,128]{2,1,0:T(8,128)S(1)}, f32[4,16,128]{2,1,0:T(8,128)S(1)}, u32[]{:S(2)}, u32[]{:S(2)}) collective-permute-start(f32[4,16,128]{2,1,0:T(8,128)S(1)} %get-tuple-element.12), channel_id=1, source_target_pairs={{0,32},{1,2},{2,1},{3,4},{4,3},{5,6},{6,5},{7,8},{8,7},{9,10},{10,... | collective-permute-start | bytes 98312 | tf_op jit(solution)/shard_map/ppermute | solution.py:387
  19.0 0.0 collective-permute-start
  19.0 0.0 collective-permute-done.2.core
  19.0 0.0 collective-permute-done.3.chip
  19.0 2.2 %place_spheres.1.dots = f32[18,2,2,16,128]{4,3,2,1,0:T(8,128)S(1)} custom-call(f32[8,7040]{1,0:T(8,128)S(1)} %get-tuple-element.13.own, f32[8,7040]{1,0:T(8,128)S(1)} %collective-permute-done.2.core, f32[8,7040]{1,0:T(8,128)S(1)} %collective-permute-done.3.chip), custom_call_target="tpu_custom_call" | custom-call | tf_op jit(solution)/shard_map/place_spheres/pallas_call | solution.py:388
  21.3 1.6 %collective-permute-done.4.second = f32[8,1280]{1,0:T(8,128)S(1)} collective-permute-done((f32[8,1280]{1,0:T(8,128)S(1)}, f32[8,1280]{1,0:T(8,128)S(1)}, u32[]{:S(2)}, u32[]{:S(2)}) %collective-permute-start.4) | collective-permute-done | bytes 40992 | tf_op jit(solution)/shard_map/ppermute | solution.py:380
  22.8 0.0 collective-permute-done.core
  22.8 0.0 collective-permute-done.1.chip
  22.8 2.1 %potential_of.1 = f32[8,6,12,128]{3,2,1,0:T(8,128)S(1)} custom-call(f32[6,16,128]{2,1,0:T(8,128)S(1)} %get-tuple-element.10.own, f32[2,16,128]{2,1,0:T(8,128)S(1)} %collective-permute-done.core, f32[4,16,128]{2,1,0:T(8,128)S(1)} %collective-permute-done.1.chip, f32[18,2,2,16,128]{4,3,2,1,0:T(8,128)S(1)} %place_spheres.1.dots, ...), custom_call_target="tpu_custom_call" | custom-call | tf_op jit(solution)/shard_map/potential_of/pallas_call | solution.py:401
  24.9 13.8 %all_to_all.10 = f32[8,6,12,128]{3,2,1,0:T(8,128)S(1)} all-to-all(f32[8,6,12,128]{3,2,1,0:T(8,128)S(1)} %potential_of.1), channel_id=1, replica_groups=mesh['band'=8,'dom'=32] {'band'}, dimensions={0} | all-to-all | bytes 589824 | tf_op jit(solution)/shard_map/all_to_all | solution.py:417
  38.7 0.7 %reshape.7 = f32[6,96,128]{2,1,0:T(8,128)} reshape(f32[6,8,12,128]{3,2,1,0:T(8,128)S(1)} %copy.6) | data formatting | bytes 589824 | tf_op jit(solution)/shard_map/reshape | solution.py:418
  (2 shorter events, 0.1 us)
Async XLA Ops:
  0.0 1.0 %copy-start.1 = (f32[1,6,96,128]{3,2,1,0:T(8,128)S(1)}, f32[1,6,96,128]{3,2,1,0:T(8,128)}, u32[]{:S(2)}) copy-start(f32[1,6,96,128]{3,2,1,0:T(8,128)} %cells.1) | copy-start | bytes 884740
  1.0 6.6 %copy-start = (bf16[8,9,6912]{2,0,1:T(8,128)(2,1)S(1)}, bf16[8,9,6912]{2,0,1:T(8,128)(2,1)}, u32[]{:S(2)}) copy-start(bf16[8,9,6912]{2,0,1:T(8,128)(2,1)} %param.7) | copy-start | bytes 2985988
  1.7 13.6 %all-to-all-start = ((f32[8,6,16,128]{3,2,1,0:T(8,128)}), f32[8,6,16,128]{3,2,1,0:T(8,128)S(1)}, u32[]{:S(2)}, u32[]{:S(2)}) async-start(f32[8,6,16,128]{3,2,1,0:T(8,128)} %windows.1), calls=%async_computation | async-start | bytes 786432 | tf_op jit(solution)/shard_map/all_to_all | solution.py:371
  7.5 0.7 %copy-start.3 = (bf16[9,8]{0,1:T(8,128)(2,1)S(1)}, bf16[9,8]{0,1:T(8,128)(2,1)}, u32[]{:S(2)}) copy-start(bf16[9,8]{0,1:T(8,128)(2,1)} %param.6) | copy-start | bytes 436
  7.5 0.7 %copy-start.2 = (s32[3,8]{1,0:T(4,128)S(1)}, s32[3,8]{1,0:T(4,128)}, u32[]{:S(2)}) copy-start(s32[3,8]{1,0:T(4,128)} %offsets.1) | copy-start | bytes 292
  8.6 10.5 %collective-permute-start.2 = (f32[8,7040]{1,0:T(8,128)S(1)}, f32[8,7040]{1,0:T(8,128)S(1)}, u32[]{:S(2)}, u32[]{:S(2)}) collective-permute-start(f32[8,7040]{1,0:T(8,128)S(1)} %get-tuple-element.13.own), channel_id=1, source_target_pairs={{0,1},{1,0},{2,3},{3,2},{4,5},{5,4},{6,7},{7,6},{8,9},{9,8},{10,11... | collective-permute-start | bytes 675848 | tf_op jit(solution)/shard_map/ppermute | solution.py:379
  8.7 10.4 %collective-permute-start.3 = (f32[8,7040]{1,0:T(8,128)S(1)}, f32[8,7040]{1,0:T(8,128)S(1)}, u32[]{:S(2)}, u32[]{:S(2)}) collective-permute-start(f32[8,7040]{1,0:T(8,128)S(1)} %get-tuple-element.13.own), channel_id=1, source_target_pairs={{0,32},{1,2},{2,1},{3,4},{4,3},{5,6},{6,5},{7,8},{8,7},{9,10},{10,... | collective-permute-start | bytes 675848 | tf_op jit(solution)/shard_map/ppermute | solution.py:381
  14.9 8.0 %collective-permute-start.4 = (f32[8,1280]{1,0:T(8,128)S(1)}, f32[8,1280]{1,0:T(8,128)S(1)}, u32[]{:S(2)}, u32[]{:S(2)}) collective-permute-start(f32[8,1280]{1,0:T(8,128)S(1)} %get-tuple-element.14), channel_id=1, source_target_pairs={{0,2},{1,3},{2,4},{3,5},{4,6},{5,7},{6,8},{7,9},{8,10},{9,11},{10,... | collective-permute-start | bytes 122888 | tf_op jit(solution)/shard_map/ppermute | solution.py:380
  15.3 7.5 %collective-permute-start.1 = (f32[4,16,128]{2,1,0:T(8,128)S(1)}, f32[4,16,128]{2,1,0:T(8,128)S(1)}, u32[]{:S(2)}, u32[]{:S(2)}) collective-permute-start(f32[4,16,128]{2,1,0:T(8,128)S(1)} %get-tuple-element.12), channel_id=1, source_target_pairs={{0,32},{1,2},{2,1},{3,4},{4,3},{5,6},{6,5},{7,8},{8,7},{9,10},{10,... | collective-permute-start | bytes 98312 | tf_op jit(solution)/shard_map/ppermute | solution.py:387
  19.0 3.8 %collective-permute-start = (f32[2,16,128]{2,1,0:T(8,128)S(1)}, f32[2,16,128]{2,1,0:T(8,128)S(1)}, u32[]{:S(2)}, u32[]{:S(2)}) collective-permute-start(f32[2,16,128]{2,1,0:T(8,128)S(1)} %get-tuple-element.11), channel_id=1, source_target_pairs={{0,1},{1,0},{2,3},{3,2},{4,5},{5,4},{6,7},{7,6},{8,9},{9,8},{10,11... | collective-permute-start | bytes 49160 | tf_op jit(solution)/shard_map/ppermute | solution.py:386

commit v4 on v3

--- a/solution.py
+++ b/solution.py
@@ -97,47 +97,53 @@
     return jnp.where(lane == 1, jnp.where(counts(row), there, FAR), whole)
 
 
-def spread_blocks(sources, flat, total, info):
+def spread_blocks(groups, flat, total, info, chosen):
     column = lax.broadcasted_iota(jnp.int32, (256, 256), 1)
     line = lax.rem(lax.broadcasted_iota(jnp.int32, (256, 256), 0), 128)
     inner_z = jnp.where(column < 128, 2 * column, 2 * column - 255) - line
     inner_z = jnp.where(line < SBZ, inner_z, -1)
     row_y = lax.broadcasted_iota(jnp.int32, (32, 128), 0)
-    for which, (depth_x, first_plane, begin) in enumerate(sources):
-
-        def one(slot, carry):
-            col = info[which, slot, 1]
-
-            @pl.when((col > 0) & (col < 56))
-            def _():
-                row = info[which, slot, 0]
-                depth = info[which, slot, 2]
-                shift = lax.rem(col, 8)
-                base = pl.multiple_of(col - shift, 8)
-                held = (row_y >= shift) & (row_y < shift + SBY)
-                parts = []
-                for x in range(depth_x):
-                    start = 64 + ((begin + x) * SBY - shift) * SLOTS + slot
-                    parts.append(jnp.where(held, flat[pl.ds(start, 32, stride=SLOTS), :], 0.0))
-                block = jnp.concatenate(parts, axis=0)
-                high = block.astype(jnp.bfloat16)
-                low = (block - high.astype(jnp.float32)).astype(jnp.bfloat16)
-                pick = jnp.where(inner_z == depth, 1.0, 0.0).astype(jnp.bfloat16)
-                both = jnp.concatenate([high, low], axis=1)
-                spread = jnp.dot(both, pick, preferred_element_type=jnp.float32)
-                planes = pl.ds(row + first_plane, depth_x)
-                rows = pl.ds(base, 32)
-                spread = spread.reshape(depth_x, 32, 256)
-                for odd_z in range(2):
-                    half = spread[:, :, 128 * odd_z : 128 * odd_z + 128]
-                    total[odd_z, planes, rows, :] = total[odd_z, planes, rows, :] + half
-
+    for first_source, sources, depth_x, first_plane, begin in groups:
+        count = jnp.int32(0)
+        for which in range(sources):
+            for slot in range(SLOTS):
+                col = info[first_source + which, slot, 1]
+                chosen[count] = which * SLOTS + slot
+                count = count + jnp.where((col > 0) & (col < 56), 1, 0)
+
+        def one(index, carry):
+            both = chosen[index]
+            source = lax.shift_right_logical(both, 3)
+            slot = both & (SLOTS - 1)
+            row = info[first_source + source, slot, 0]
+            col = info[first_source + source, slot, 1]
+            depth = info[first_source + source, slot, 2]
+            shift = lax.rem(col, 8)
+            base = pl.multiple_of(col - shift, 8)
+            held = (row_y >= shift) & (row_y < shift + SBY)
+            origin = 64 + ((begin + SBX * source) * SBY - shift) * SLOTS + slot
+            parts = []
+            for x in range(depth_x):
+                start = origin + x * SBY * SLOTS
+                parts.append(jnp.where(held, flat[pl.ds(start, 32, stride=SLOTS), :], 0.0))
+            block = jnp.concatenate(parts, axis=0)
+            high = block.astype(jnp.bfloat16)
+            low = (block - high.astype(jnp.float32)).astype(jnp.bfloat16)
+            pick = jnp.where(inner_z == depth, 1.0, 0.0).astype(jnp.bfloat16)
+            terms = jnp.concatenate([high, low], axis=1)
+            spread = jnp.dot(terms, pick, preferred_element_type=jnp.float32)
+            planes = pl.ds(row + first_plane - FX * source, depth_x)
+            rows = pl.ds(base, 32)
+            spread = spread.reshape(depth_x, 32, 256)
+            for odd_z in range(2):
+                half = spread[:, :, 128 * odd_z : 128 * odd_z + 128]
+                total[odd_z, planes, rows, :] = total[odd_z, planes, rows, :] + half
             return carry
 
-        lax.fori_loop(0, SLOTS, one, 0)
-
-
-def place_kernel(own, core, chip, out, flat, total, whole, info, sem):
+        lax.fori_loop(0, count, one, 0)
+
+
+def place_kernel(own, core, chip, out, flat, total, whole, info, chosen, sem):
     slab = lax.axis_index("dom")
     even_slab = lax.rem(slab, 2) == 0
     last = lax.axis_size("dom") - 1
@@ -167,7 +173,7 @@
     line_up(before_tile, SBX, SBX, flat)
     line_up(after_tile, 3, 2 * SBX, flat)
     copy.wait()
-    spread_blocks([(SBX, 14, 0), (SBX, 2, SBX), (3, 26, 2 * SBX)], flat, total, info)
+    spread_blocks([(0, 2, SBX, 14, 0), (2, 1, 3, 26, 2 * SBX)], flat, total, info, chosen)
     for plane in range(FX + 6):
         for odd_y in range(2):
             for odd_z in range(2):
@@ -187,7 +193,7 @@
     send_chip[2:4] = own[2:4]
 
 
-def main_kernel(own, core, chip, dots, second, out, dens, flux_x, value, flat, total, whole, info, sem):
+def main_kernel(own, core, chip, dots, second, out, dens, flux_x, value, flat, total, whole, info, chosen, sem):
     slab = lax.axis_index("dom")
     part = lax.axis_index("band")
     last = lax.axis_size("dom") - 1
@@ -243,9 +249,6 @@
             return slab < last
         return None
 
-    copy.wait()
-    spread_blocks([(2, -10, 0)], flat, total, info)
-
     grids = {}
     for plane in range(-3, FX + 3):
         index, odd = plane // 2, plane % 2
@@ -261,9 +264,15 @@
             for odd_z in range(2):
                 cells = 0.75 * grids[index][odd_y][odd_z] + 0.25 * grids[near][odd_y][odd_z]
                 cells = cells + dots[plane + 3, odd_y, odd_z]
-                if plane < -1:
-                    cells = cells + total[odd_z, plane + 4, pl.ds(24 + odd_y, WY, stride=2), :]
                 dens[plane + 3, odd_y, odd_z] = jnp.where(ok, cells, 0.0)
+
+    copy.wait()
+    spread_blocks([(0, 1, 2, -10, 0)], flat, total, info, chosen)
+    for plane in range(2):
+        for odd_y in range(2):
+            for odd_z in range(2):
+                cells = total[odd_z, plane + 1, pl.ds(24 + odd_y, WY, stride=2), :]
+                dens[plane, odd_y, odd_z] = dens[plane, odd_y, odd_z] + jnp.where(inside, cells, 0.0)
 
     def density(plane):
         return [[dens[plane + 3, odd_y, odd_z] for odd_z in range(2)] for odd_y in range(2)]
@@ -330,8 +339,14 @@
                 rows.append(0.125 * low + 0.375 * mid)
             depth[odd_z] = 0.125 * (row_before(rows[1]) + row_after(rows[0])) + 0.375 * (rows[0] + rows[1])
         cells = 0.125 * (lane_before(depth[1]) + lane_after(depth[0])) + 0.375 * (depth[0] + depth[1])
-        for copy in range(PARTS):
-            out[copy, index] = cells[RIM : RIM + YB]
+        for part_to in range(PARTS):
+            out[part_to, YB * index : YB * index + YB] = cells[RIM : RIM + YB]
+
+
+def join_kernel(pieces, out):
+    for part in range(PARTS):
+        for index in range(CX):
+            out[index, YB * part : YB * part + YB] = pieces[part, YB * index : YB * index + YB]
 
 
 SMEM = pl.BlockSpec(memory_space=pltpu.SMEM)
@@ -395,13 +410,14 @@
             pltpu.VMEM((2, 41, 80, CZ), F32),
             pltpu.VMEM((3, SLOTS, 128), jnp.int32),
             pltpu.SMEM((3, SLOTS, 128), jnp.int32),
+            pltpu.SMEM((3 * SLOTS,), jnp.int32),
             pltpu.SemaphoreType.DMA,
         ],
     )(packed, dots_core, dots_chip)
     result = call(
         main_kernel,
         "potential_of",
-        (PARTS, CX, YB, CZ),
+        (PARTS, CX * YB, CZ),
         [VMEM] * 5,
         [
             pltpu.VMEM((FX + 6, 2, 2, WY, CZ), F32),
@@ -411,11 +427,12 @@
             pltpu.VMEM((2, 4, 80, CZ), F32),
             pltpu.VMEM((1, SLOTS, 128), jnp.int32),
             pltpu.SMEM((1, SLOTS, 128), jnp.int32),
+            pltpu.SMEM((3 * SLOTS,), jnp.int32),
             pltpu.SemaphoreType.DMA,
         ],
     )(own, core, chip, dots, dots_second)
     gathered = lax.all_to_all(result, "band", 0, 0)
-    return gathered.transpose(1, 0, 2, 3).reshape(CX, PARTS * YB, CZ)
+    return call(join_kernel, "join", (CX, PARTS * YB, CZ), [VMEM])(gathered)
 
 
 def solution(mesh):

time: 39.7 us -> 39.2 us (0.987)
  local copies, waits for them, and re-layouts: 2.41 us -> 1.64 us
  waiting for transfers between devices: 2.01 us -> 2.46 us
    reshape x1 -> x0, local copies, waits for them, and re-layouts: 0.74 us -> none  [body(): return gathered.transpose(1, 0, 2, 3).reshape(CX, PARTS * YB, CZ)]
    pallas_call x1 -> x2, Pallas kernels: 2.12 us -> 2.59 us  [the longest x1 1.85 us: body(): call(main_kernel, 'potential_of', (PARTS, CX * YB, CZ), [VMEM] * 5, [pltp...]
    pallas_call x1, Pallas kernels: 2.22 us -> 1.77 us  [body(): call(place_kernel, 'place_spheres', (FX + 6, 2, 2, WY, CZ), [VMEM] * 3, [...]
    ppermute x1, waiting for transfers between devices: 1.56 us -> 2.01 us  [body(): dots_second = lax.ppermute(tail, 'dom', second)]
  transfers between devices with their start and end apart: 6 -> 6, of which waited for: 2 -> 2; matrix products, arithmetic and copies ran while one was open for 0% -> 0% of each run, Pallas kernels for 7% -> 6%
where the time goes in v4:
time: 39.2 us; the launch traced here: 39 us
  starting transfers between devices  15.1 us (39%)
  blocking collectives  13.6 us (35%)
  Pallas kernels  5.51 us (14%)
  waiting for transfers between devices  2.46 us (6%)
  local copies, waits for them, and re-layouts  1.64 us (4%)
  between operations  0.72 us (2%)
    all_to_all x1, blocking collectives, body(): gathered = lax.all_to_all(result, 'band', 0, 0)  13.6 us
    ppermute x1, starting transfers between devices, body(): dots_chip = lax.ppermute(packed, ('band', 'dom'), chip_pairs)  6.19 us
    all_to_all x1, starting transfers between devices, body(): windows = lax.all_to_all(windows, 'band', 0, 0)  5.1 us
    ppermute x1, starting transfers between devices, body(): chip = lax.ppermute(send_chip, ('band', 'dom'), chip_pairs)  3.68 us
    ppermute x1, waiting for transfers between devices, body(): dots_second = lax.ppermute(tail, 'dom', second)  2.01 us
    pallas_call x1, Pallas kernels, body(): call(main_kernel, 'potential_of', (PARTS, CX * YB, CZ), [VMEM] * 5, [pltp...  1.85 us
    pallas_call x1, Pallas kernels, body(): call(place_kernel, 'place_spheres', (FX + 6, 2, 2, WY, CZ), [VMEM] * 3, [...  1.77 us
    unnamed x8, local copies, waits for them, and re-layouts  1.64 us
  transfers between devices with their start and end apart: 6, of which 2 were waited for; matrix products, arithmetic and copies ran while one was open for 0% of the time, Pallas kernels for 6%

profile of v4, /device:TPU:4, one launch (start us, length us, event | category | flops | bytes accessed | tf_op | source)
XLA Modules:
  0.0 39.0 jit_solution(12633140982621061433)
XLA Ops:
  0.0 0.0 copy-start.1
  0.0 1.0 %copy-done.1 = f32[1,6,96,128]{3,2,1,0:T(8,128)S(1)} copy-done((f32[1,6,96,128]{3,2,1,0:T(8,128)S(1)}, f32[1,6,96,128]{3,2,1,0:T(8,128)}, u32[]{:S(2)}) %copy-start.1) | copy-done | bytes 294936
  1.0 0.0 copy-start
  1.0 0.8 %windows.1 = f32[8,6,16,128]{3,2,1,0:T(8,128)} custom-call(f32[1,6,96,128]{3,2,1,0:T(8,128)S(1)} %copy-done.1), custom_call_target="tpu_custom_call" | custom-call | tf_op jit(solution)/shard_map/windows/pallas_call | solution.py:385
  1.7 5.1 %all-to-all-start = ((f32[8,6,16,128]{3,2,1,0:T(8,128)}), f32[8,6,16,128]{3,2,1,0:T(8,128)S(1)}, u32[]{:S(2)}, u32[]{:S(2)}) async-start(f32[8,6,16,128]{3,2,1,0:T(8,128)} %windows.1), calls=%async_computation | async-start | bytes 786432 | tf_op jit(solution)/shard_map/all_to_all | solution.py:386
  7.5 0.0 copy-start.3
  7.5 0.0 copy-start.2
  7.5 0.0 copy-done
  7.5 0.7 %copy-done.3 = bf16[9,8]{0,1:T(8,128)(2,1)S(1)} copy-done((bf16[9,8]{0,1:T(8,128)(2,1)S(1)}, bf16[9,8]{0,1:T(8,128)(2,1)}, u32[]{:S(2)}) %copy-start.3) | copy-done | bytes 168
  8.2 0.0 copy-done.2
  8.2 0.4 blocks.1
  8.6 0.1 collective-permute-start.2
  8.7 6.2 %collective-permute-start.3 = (f32[8,7040]{1,0:T(8,128)S(1)}, f32[8,7040]{1,0:T(8,128)S(1)}, u32[]{:S(2)}, u32[]{:S(2)}) collective-permute-start(f32[8,7040]{1,0:T(8,128)S(1)} %get-tuple-element.13.own), channel_id=1, source_target_pairs={{0,32},{1,2},{2,1},{3,4},{4,3},{5,6},{6,5},{7,8},{8,7},{9,10},{10,... | collective-permute-start | bytes 675848 | tf_op jit(solution)/shard_map/ppermute | solution.py:396
  14.9 0.0 collective-permute-start.4
  14.9 0.4 %all-to-all-done.windows = f32[8,6,16,128]{3,2,1,0:T(8,128)S(1)} async-done(((f32[8,6,16,128]{3,2,1,0:T(8,128)}), f32[8,6,16,128]{3,2,1,0:T(8,128)S(1)}, u32[]{:S(2)}, u32[]{:S(2)}) %all-to-all-start) | async-done | bytes 393248 | tf_op jit(solution)/shard_map/all_to_all | solution.py:386
  15.3 3.7 %collective-permute-start.1 = (f32[4,16,128]{2,1,0:T(8,128)S(1)}, f32[4,16,128]{2,1,0:T(8,128)S(1)}, u32[]{:S(2)}, u32[]{:S(2)}) collective-permute-start(f32[4,16,128]{2,1,0:T(8,128)S(1)} %get-tuple-element.12), channel_id=1, source_target_pairs={{0,32},{1,2},{2,1},{3,4},{4,3},{5,6},{6,5},{7,8},{8,7},{9,10},{10,... | collective-permute-start | bytes 98312 | tf_op jit(solution)/shard_map/ppermute | solution.py:402
  19.0 0.0 collective-permute-start
  19.0 0.0 collective-permute-done.2.core
  19.0 0.0 collective-permute-done.3.chip
  19.0 1.8 %place_spheres.1.dots = f32[18,2,2,16,128]{4,3,2,1,0:T(8,128)S(1)} custom-call(f32[8,7040]{1,0:T(8,128)S(1)} %get-tuple-element.13.own, f32[8,7040]{1,0:T(8,128)S(1)} %collective-permute-done.2.core, f32[8,7040]{1,0:T(8,128)S(1)} %collective-permute-done.3.chip), custom_call_target="tpu_custom_call" | custom-call | tf_op jit(solution)/shard_map/place_spheres/pallas_call | solution.py:403
  20.8 2.0 %collective-permute-done.4.second = f32[8,1280]{1,0:T(8,128)S(1)} collective-permute-done((f32[8,1280]{1,0:T(8,128)S(1)}, f32[8,1280]{1,0:T(8,128)S(1)}, u32[]{:S(2)}, u32[]{:S(2)}) %collective-permute-start.4) | collective-permute-done | bytes 40992 | tf_op jit(solution)/shard_map/ppermute | solution.py:395
  22.8 0.0 collective-permute-done.core
  22.8 0.0 collective-permute-done.1.chip
  22.8 1.8 %potential_of.1 = f32[8,72,128]{2,1,0:T(8,128)S(1)} custom-call(f32[6,16,128]{2,1,0:T(8,128)S(1)} %get-tuple-element.10.own, f32[2,16,128]{2,1,0:T(8,128)S(1)} %collective-permute-done.core, f32[4,16,128]{2,1,0:T(8,128)S(1)} %collective-permute-done.1.chip, f32[18,2,2,16,128]{4,3,2,1,0:T(8,128)S(1)} %place_spheres.1.dots, ...), custom_call_target="tpu_custom_call" | custom-call | tf_op jit(solution)/shard_map/potential_of/pallas_call | solution.py:417
  24.7 13.6 %all_to_all.10.pieces = f32[8,72,128]{2,1,0:T(8,128)S(1)} all-to-all(f32[8,72,128]{2,1,0:T(8,128)S(1)} %potential_of.1), channel_id=1, replica_groups=mesh['band'=8,'dom'=32] {'band'}, dimensions={0} | all-to-all | bytes 589824 | tf_op jit(solution)/shard_map/all_to_all | solution.py:434
  38.3 0.7 %join.1 = f32[6,96,128]{2,1,0:T(8,128)} custom-call(f32[8,72,128]{2,1,0:T(8,128)S(1)} %all_to_all.10.pieces), custom_call_target="tpu_custom_call" | custom-call | tf_op jit(solution)/shard_map/join/pallas_call | solution.py:435
  (1 shorter events, 0.0 us)
Async XLA Ops:
  0.0 1.0 %copy-start.1 = (f32[1,6,96,128]{3,2,1,0:T(8,128)S(1)}, f32[1,6,96,128]{3,2,1,0:T(8,128)}, u32[]{:S(2)}) copy-start(f32[1,6,96,128]{3,2,1,0:T(8,128)} %cells.1) | copy-start | bytes 884740
  1.0 6.6 %copy-start = (bf16[8,9,6912]{2,0,1:T(8,128)(2,1)S(1)}, bf16[8,9,6912]{2,0,1:T(8,128)(2,1)}, u32[]{:S(2)}) copy-start(bf16[8,9,6912]{2,0,1:T(8,128)(2,1)} %param.7) | copy-start | bytes 2985988
  1.7 13.6 %all-to-all-start = ((f32[8,6,16,128]{3,2,1,0:T(8,128)}), f32[8,6,16,128]{3,2,1,0:T(8,128)S(1)}, u32[]{:S(2)}, u32[]{:S(2)}) async-start(f32[8,6,16,128]{3,2,1,0:T(8,128)} %windows.1), calls=%async_computation | async-start | bytes 786432 | tf_op jit(solution)/shard_map/all_to_all | solution.py:386
  7.5 0.7 %copy-start.3 = (bf16[9,8]{0,1:T(8,128)(2,1)S(1)}, bf16[9,8]{0,1:T(8,128)(2,1)}, u32[]{:S(2)}) copy-start(bf16[9,8]{0,1:T(8,128)(2,1)} %param.6) | copy-start | bytes 436
  7.5 0.7 %copy-start.2 = (s32[3,8]{1,0:T(4,128)S(1)}, s32[3,8]{1,0:T(4,128)}, u32[]{:S(2)}) copy-start(s32[3,8]{1,0:T(4,128)} %offsets.1) | copy-start | bytes 292
  8.6 10.5 %collective-permute-start.2 = (f32[8,7040]{1,0:T(8,128)S(1)}, f32[8,7040]{1,0:T(8,128)S(1)}, u32[]{:S(2)}, u32[]{:S(2)}) collective-permute-start(f32[8,7040]{1,0:T(8,128)S(1)} %get-tuple-element.13.own), channel_id=1, source_target_pairs={{0,1},{1,0},{2,3},{3,2},{4,5},{5,4},{6,7},{7,6},{8,9},{9,8},{10,11... | collective-permute-start | bytes 675848 | tf_op jit(solution)/shard_map/ppermute | solution.py:394
  8.7 10.4 %collective-permute-start.3 = (f32[8,7040]{1,0:T(8,128)S(1)}, f32[8,7040]{1,0:T(8,128)S(1)}, u32[]{:S(2)}, u32[]{:S(2)}) collective-permute-start(f32[8,7040]{1,0:T(8,128)S(1)} %get-tuple-element.13.own), channel_id=1, source_target_pairs={{0,32},{1,2},{2,1},{3,4},{4,3},{5,6},{6,5},{7,8},{8,7},{9,10},{10,... | collective-permute-start | bytes 675848 | tf_op jit(solution)/shard_map/ppermute | solution.py:396
  14.9 8.0 %collective-permute-start.4 = (f32[8,1280]{1,0:T(8,128)S(1)}, f32[8,1280]{1,0:T(8,128)S(1)}, u32[]{:S(2)}, u32[]{:S(2)}) collective-permute-start(f32[8,1280]{1,0:T(8,128)S(1)} %get-tuple-element.14), channel_id=1, source_target_pairs={{0,2},{1,3},{2,4},{3,5},{4,6},{5,7},{6,8},{7,9},{8,10},{9,11},{10,... | collective-permute-start | bytes 122888 | tf_op jit(solution)/shard_map/ppermute | solution.py:395
  15.3 7.5 %collective-permute-start.1 = (f32[4,16,128]{2,1,0:T(8,128)S(1)}, f32[4,16,128]{2,1,0:T(8,128)S(1)}, u32[]{:S(2)}, u32[]{:S(2)}) collective-permute-start(f32[4,16,128]{2,1,0:T(8,128)S(1)} %get-tuple-element.12), channel_id=1, source_target_pairs={{0,32},{1,2},{2,1},{3,4},{4,3},{5,6},{6,5},{7,8},{8,7},{9,10},{10,... | collective-permute-start | bytes 98312 | tf_op jit(solution)/shard_map/ppermute | solution.py:402
  19.0 3.8 %collective-permute-start = (f32[2,16,128]{2,1,0:T(8,128)S(1)}, f32[2,16,128]{2,1,0:T(8,128)S(1)}, u32[]{:S(2)}, u32[]{:S(2)}) collective-permute-start(f32[2,16,128]{2,1,0:T(8,128)S(1)} %get-tuple-element.11), channel_id=1, source_target_pairs={{0,1},{1,0},{2,3},{3,2},{4,5},{5,4},{6,7},{7,6},{8,9},{9,8},{10,11... | collective-permute-start | bytes 49160 | tf_op jit(solution)/shard_map/ppermute | solution.py:401

commit v5 on v4

--- a/solution.py
+++ b/solution.py
@@ -45,7 +45,7 @@
         windows[part] = rows
 
 
-def blocks_kernel(offsets, count, moments, shapes, packed, tail):
+def blocks_kernel(offsets, count, moments, shapes, packed):
     row = lax.broadcasted_iota(jnp.int32, (SLOTS, SLOTS), 0)
     lane = lax.broadcasted_iota(jnp.int32, (SLOTS, SLOTS), 1)
     slot = lax.broadcasted_iota(jnp.int32, (SLOTS, 1), 0)
@@ -69,7 +69,6 @@
                 jnp.float32
             )
         packed[:, lanes] = total
-    tail[...] = packed[:, BLOCK + 128 - TAIL :]
 
 
 def line_up(read, depth_x, begin, flat):
@@ -181,29 +180,46 @@
                 out[plane, odd_y, odd_z] = total[odd_z, plane + 11, rows, :]
 
 
-def own_kernel(windows, own, send_core, send_chip):
+def own_kernel(windows, other, own, send_chip):
     for plane in range(CX):
         cells = windows[0, plane]
         for part in range(1, PARTS):
             cells = cells + windows[part, plane]
         own[plane] = cells
     even_slab = lax.rem(lax.axis_index("dom"), 2) == 0
-    send_core[...] = jnp.where(even_slab, own[CX - 2 : CX], own[0:2])
     send_chip[0:2] = jnp.where(even_slab, own[0:2], own[CX - 2 : CX])
-    send_chip[2:4] = own[2:4]
-
-
-def main_kernel(own, core, chip, dots, second, out, dens, flux_x, value, flat, total, whole, info, chosen, sem):
+    put_tail(other, send_chip)
+
+
+def edge_kernel(own, other, send_core):
+    even_slab = lax.rem(lax.axis_index("dom"), 2) == 0
+    send_core[0:2] = jnp.where(even_slab, own[CX - 2 : CX], own[0:2])
+    put_tail(other, send_core)
+
+
+def put_tail(packed, out):
+    for tile in range(TAIL // 128):
+        first = BLOCK + 128 - TAIL + 128 * tile
+        rows = pl.ds(SLOTS * (tile % 2), SLOTS)
+        out[2 + tile // 2, rows] = packed[:, first : first + 128]
+
+
+def main_kernel(own, core, chip, dots, out, dens, flux_x, value, flat, total, whole, info, chosen, sem):
     slab = lax.axis_index("dom")
     part = lax.axis_index("band")
     last = lax.axis_size("dom") - 1
     even_slab = lax.rem(slab, 2) == 0
-    whole[0] = whole_offsets(second[:, pl.ds(TAIL - 128, 128)], lambda row: (row >= 10) & (slab > 1))
+
+    def second(tile):
+        rows = pl.ds(SLOTS * (tile % 2), SLOTS)
+        return jnp.where(even_slab, chip[2 + tile // 2, rows], core[2 + tile // 2, rows])
+
+    whole[0] = whole_offsets(second(TAIL // 128 - 1), lambda row: (row >= 10) & (slab > 1))
     copy = pltpu.make_async_copy(whole, info, sem)
     copy.start()
     for odd_z in range(2):
         total[odd_z, pl.ds(0, 4), pl.ds(24, 32), :] = jnp.zeros((4, 32, CZ), jnp.float32)
-    line_up(lambda tile: second[:, 128 * tile : 128 * tile + 128], 2, 0, flat)
+    line_up(second, 2, 0, flat)
     lane = lax.broadcasted_iota(jnp.int32, (WY, CZ), 1)
     first_lane = lane == 0
     last_lane = lane == CZ - 1
@@ -374,7 +390,6 @@
 def body(partial_density, moments, shape_functions, sphere_offsets, owned_count):
     slabs = lax.axis_size("dom")
     core_pairs = [(i, i ^ 1) for i in range(slabs)]
-    second = [(i, (i + 2) % slabs) for i in range(slabs)]
     chip_pairs = []
     for b in range(PARTS):
         for i in range(slabs):
@@ -385,21 +400,22 @@
     windows = call(windows_kernel, "windows", (PARTS, CX, WY, CZ), [VMEM])(partial_density)
     windows = lax.all_to_all(windows, "band", 0, 0)
 
-    packed, tail = call(
+    packed = call(
         blocks_kernel,
         "blocks",
-        ((SLOTS, BLOCK + 128), (SLOTS, TAIL)),
+        (SLOTS, BLOCK + 128),
         [VMEM] * 4,
     )(sphere_offsets, owned_count.reshape(1, 1), moments.T, shape_functions.transpose(1, 0, 2))
     dots_core = lax.ppermute(packed, "dom", core_pairs)
-    dots_second = lax.ppermute(tail, "dom", second)
     dots_chip = lax.ppermute(packed, ("band", "dom"), chip_pairs)
 
-    own, send_core, send_chip = call(
-        own_kernel, "own_window", ((CX, WY, CZ), (2, WY, CZ), (4, WY, CZ)), [VMEM]
-    )(windows)
+    rim = (2 + TAIL // 256, WY, CZ)
+    own, send_chip = call(own_kernel, "own_window", ((CX, WY, CZ), rim), [VMEM] * 2)(
+        windows, dots_core
+    )
+    chip = lax.ppermute(send_chip, ("band", "dom"), chip_pairs)
+    send_core = call(edge_kernel, "edge", rim, [VMEM] * 2)(own, dots_chip)
     core = lax.ppermute(send_core, "dom", core_pairs)
-    chip = lax.ppermute(send_chip, ("band", "dom"), chip_pairs)
     dots = call(
         place_kernel,
         "place_spheres",
@@ -418,7 +434,7 @@
         main_kernel,
         "potential_of",
         (PARTS, CX * YB, CZ),
-        [VMEM] * 5,
+        [VMEM] * 4,
         [
             pltpu.VMEM((FX + 6, 2, 2, WY, CZ), F32),
             pltpu.VMEM((FX + 4, 2, 2, WY, CZ), F32),
@@ -430,7 +446,7 @@
             pltpu.SMEM((3 * SLOTS,), jnp.int32),
             pltpu.SemaphoreType.DMA,
         ],
-    )(own, core, chip, dots, dots_second)
+    )(own, core, chip, dots)
     gathered = lax.all_to_all(result, "band", 0, 0)
     return call(join_kernel, "join", (CX, PARTS * YB, CZ), [VMEM])(gathered)
 

time: 39.2 us -> 43.3 us (1.10)
  starting transfers between devices: 15.1 us -> 16.9 us
  waiting for transfers between devices: 2.46 us -> 3.64 us
  Pallas kernels: 5.51 us -> 6.39 us
    ppermute x1, waiting for transfers between devices: 0.01 us -> 3.19 us  [body(): dots_chip = lax.ppermute(packed, ('band', 'dom'), chip_pairs)]
    ppermute x1 -> x0, waiting for transfers between devices: 2.01 us -> none  [body(): dots_second = lax.ppermute(tail, 'dom', second)]
    ppermute x1, starting transfers between devices: 3.68 us -> 5.44 us  [body(): chip = lax.ppermute(send_chip, ('band', 'dom'), chip_pairs)]
    pallas_call x1, Pallas kernels: 1.77 us -> 2.43 us  [body(): call(place_kernel, 'place_spheres', (FX + 6, 2, 2, WY, CZ), [VMEM] * 3, [...]
    pallas_call x3 -> x4, Pallas kernels: 2.23 us -> 2.45 us  [the longest x1 2.05 us: body(): call(main_kernel, 'potential_of', (PARTS, CX * YB, CZ), [VMEM] * 4, [pltp...]
  transfers between devices with their start and end apart: 6 -> 5, of which waited for: 2 -> 2; matrix products, arithmetic and copies ran while one was open for 0% -> 0% of each run, Pallas kernels for 6% -> 7%
where the time goes in v5:
time: 43.3 us; the launch traced here: 43.2 us
  starting transfers between devices  16.9 us (39%)
  blocking collectives  13.8 us (32%)
  Pallas kernels  6.39 us (15%)
  waiting for transfers between devices  3.64 us (8%)
  local copies, waits for them, and re-layouts  1.64 us (4%)
  between operations  0.74 us (2%)
    all_to_all x1, blocking collectives, body(): gathered = lax.all_to_all(result, 'band', 0, 0)  13.8 us
    ppermute x1, starting transfers between devices, body(): dots_chip = lax.ppermute(packed, ('band', 'dom'), chip_pairs)  6.19 us
    ppermute x1, starting transfers between devices, body(): chip = lax.ppermute(send_chip, ('band', 'dom'), chip_pairs)  5.44 us
    all_to_all x1, starting transfers between devices, body(): windows = lax.all_to_all(windows, 'band', 0, 0)  5.1 us
    ppermute x1, waiting for transfers between devices, body(): dots_chip = lax.ppermute(packed, ('band', 'dom'), chip_pairs)  3.19 us
    pallas_call x1, Pallas kernels, body(): call(place_kernel, 'place_spheres', (FX + 6, 2, 2, WY, CZ), [VMEM] * 3, [...  2.43 us
    pallas_call x1, Pallas kernels, body(): call(main_kernel, 'potential_of', (PARTS, CX * YB, CZ), [VMEM] * 4, [pltp...  2.05 us
    unnamed x8, local copies, waits for them, and re-layouts  1.64 us
  transfers between devices with their start and end apart: 5, of which 2 were waited for; matrix products, arithmetic and copies ran while one was open for 0% of the time, Pallas kernels for 7%

profile of v5, /device:TPU:4, one launch (start us, length us, event | category | flops | bytes accessed | tf_op | source)
XLA Modules:
  0.0 43.2 jit_solution(18310766573313555191)
XLA Ops:
  0.0 0.0 copy-start.1
  0.0 1.0 %copy-done.1 = f32[1,6,96,128]{3,2,1,0:T(8,128)S(1)} copy-done((f32[1,6,96,128]{3,2,1,0:T(8,128)S(1)}, f32[1,6,96,128]{3,2,1,0:T(8,128)}, u32[]{:S(2)}) %copy-start.1) | copy-done | bytes 294936
  1.0 0.0 copy-start
  1.0 0.8 %windows.1 = f32[8,6,16,128]{3,2,1,0:T(8,128)} custom-call(f32[1,6,96,128]{3,2,1,0:T(8,128)S(1)} %copy-done.1), custom_call_target="tpu_custom_call" | custom-call | tf_op jit(solution)/shard_map/windows/pallas_call | solution.py:400
  1.7 5.1 %all-to-all-start = ((f32[8,6,16,128]{3,2,1,0:T(8,128)}), f32[8,6,16,128]{3,2,1,0:T(8,128)S(1)}, u32[]{:S(2)}, u32[]{:S(2)}) async-start(f32[8,6,16,128]{3,2,1,0:T(8,128)} %windows.1), calls=%async_computation | async-start | bytes 786432 | tf_op jit(solution)/shard_map/all_to_all | solution.py:401
  7.5 0.0 copy-start.3
  7.5 0.0 copy-start.2
  7.5 0.0 copy-done
  7.5 0.7 %copy-done.3 = bf16[9,8]{0,1:T(8,128)(2,1)S(1)} copy-done((bf16[9,8]{0,1:T(8,128)(2,1)S(1)}, bf16[9,8]{0,1:T(8,128)(2,1)}, u32[]{:S(2)}) %copy-start.3) | copy-done | bytes 168
  8.2 0.0 copy-done.2
  8.2 0.4 blocks.1.own
  8.6 0.1 collective-permute-start
  8.7 6.2 %collective-permute-start.1 = (f32[8,7040]{1,0:T(8,128)S(1)}, f32[8,7040]{1,0:T(8,128)S(1)}, u32[]{:S(2)}, u32[]{:S(2)}) collective-permute-start(f32[8,7040]{1,0:T(8,128)S(1)} %blocks.1.own), channel_id=1, source_target_pairs={{0,32},{1,2},{2,1},{3,4},{4,3},{5,6},{6,5},{7,8},{8,7},{9,10},{10,... | collective-permute-start | bytes 675848 | tf_op jit(solution)/shard_map/ppermute | solution.py:410
  14.9 0.0 collective-permute-done.other.core
  14.9 0.4 %all-to-all-done.windows = f32[8,6,16,128]{3,2,1,0:T(8,128)S(1)} async-done(((f32[8,6,16,128]{3,2,1,0:T(8,128)}), f32[8,6,16,128]{3,2,1,0:T(8,128)S(1)}, u32[]{:S(2)}, u32[]{:S(2)}) %all-to-all-start) | async-done | bytes 393248 | tf_op jit(solution)/shard_map/all_to_all | solution.py:401
  15.3 3.2 %collective-permute-done.1.other.chip = f32[8,7040]{1,0:T(8,128)S(1)} collective-permute-done((f32[8,7040]{1,0:T(8,128)S(1)}, f32[8,7040]{1,0:T(8,128)S(1)}, u32[]{:S(2)}, u32[]{:S(2)}) %collective-permute-start.1) | collective-permute-done | bytes 225312 | tf_op jit(solution)/shard_map/ppermute | solution.py:410
  18.5 0.1 collective-permute-start.2
  18.6 5.4 %collective-permute-start.3 = (f32[7,16,128]{2,1,0:T(8,128)S(1)}, f32[7,16,128]{2,1,0:T(8,128)S(1)}, u32[]{:S(2)}, u32[]{:S(2)}) collective-permute-start(f32[7,16,128]{2,1,0:T(8,128)S(1)} %get-tuple-element.8), channel_id=1, source_target_pairs={{0,32},{1,2},{2,1},{3,4},{4,3},{5,6},{6,5},{7,8},{8,7},{9,10},{10,... | collective-permute-start | bytes 172040 | tf_op jit(solution)/shard_map/ppermute | solution.py:416
  24.1 2.4 %place_spheres.1.dots = f32[18,2,2,16,128]{4,3,2,1,0:T(8,128)S(1)} custom-call(f32[8,7040]{1,0:T(8,128)S(1)} %blocks.1.own, f32[8,7040]{1,0:T(8,128)S(1)} %collective-permute-done.other.core, f32[8,7040]{1,0:T(8,128)S(1)} %collective-permute-done.1.other.chip), custom_call_target="tpu_custom_call" | custom-call | tf_op jit(solution)/shard_map/place_spheres/pallas_call | solution.py:419
  26.5 0.0 collective-permute-done.2.core
  26.5 0.0 collective-permute-done.3.chip
  26.5 2.0 %potential_of.1 = f32[8,72,128]{2,1,0:T(8,128)S(1)} custom-call(f32[6,16,128]{2,1,0:T(8,128)S(1)} %get-tuple-element.7.own, f32[7,16,128]{2,1,0:T(8,128)S(1)} %collective-permute-done.2.core, f32[7,16,128]{2,1,0:T(8,128)S(1)} %collective-permute-done.3.chip, f32[18,2,2,16,128]{4,3,2,1,0:T(8,128)S(1)} %place_spheres.1.dots), custom_call_target="tpu_custom_call" | custom-call | tf_op jit(solution)/shard_map/potential_of/pallas_call | solution.py:433
  28.6 13.8 %all_to_all.10.pieces = f32[8,72,128]{2,1,0:T(8,128)S(1)} all-to-all(f32[8,72,128]{2,1,0:T(8,128)S(1)} %potential_of.1), channel_id=1, replica_groups=mesh['band'=8,'dom'=32] {'band'}, dimensions={0} | all-to-all | bytes 589824 | tf_op jit(solution)/shard_map/all_to_all | solution.py:450
  42.4 0.7 %join.1 = f32[6,96,128]{2,1,0:T(8,128)} custom-call(f32[8,72,128]{2,1,0:T(8,128)S(1)} %all_to_all.10.pieces), custom_call_target="tpu_custom_call" | custom-call | tf_op jit(solution)/shard_map/join/pallas_call | solution.py:451
  (2 shorter events, 0.0 us)
Async XLA Ops:
  0.0 1.0 %copy-start.1 = (f32[1,6,96,128]{3,2,1,0:T(8,128)S(1)}, f32[1,6,96,128]{3,2,1,0:T(8,128)}, u32[]{:S(2)}) copy-start(f32[1,6,96,128]{3,2,1,0:T(8,128)} %cells.1) | copy-start | bytes 884740
  1.0 6.6 %copy-start = (bf16[8,9,6912]{2,0,1:T(8,128)(2,1)S(1)}, bf16[8,9,6912]{2,0,1:T(8,128)(2,1)}, u32[]{:S(2)}) copy-start(bf16[8,9,6912]{2,0,1:T(8,128)(2,1)} %param.7) | copy-start | bytes 2985988
  1.7 13.6 %all-to-all-start = ((f32[8,6,16,128]{3,2,1,0:T(8,128)}), f32[8,6,16,128]{3,2,1,0:T(8,128)S(1)}, u32[]{:S(2)}, u32[]{:S(2)}) async-start(f32[8,6,16,128]{3,2,1,0:T(8,128)} %windows.1), calls=%async_computation | async-start | bytes 786432 | tf_op jit(solution)/shard_map/all_to_all | solution.py:401
  7.5 0.7 %copy-start.3 = (bf16[9,8]{0,1:T(8,128)(2,1)S(1)}, bf16[9,8]{0,1:T(8,128)(2,1)}, u32[]{:S(2)}) copy-start(bf16[9,8]{0,1:T(8,128)(2,1)} %param.6) | copy-start | bytes 436
  7.5 0.7 %copy-start.2 = (s32[3,8]{1,0:T(4,128)S(1)}, s32[3,8]{1,0:T(4,128)}, u32[]{:S(2)}) copy-start(s32[3,8]{1,0:T(4,128)} %offsets.1) | copy-start | bytes 292
  8.6 6.3 %collective-permute-start = (f32[8,7040]{1,0:T(8,128)S(1)}, f32[8,7040]{1,0:T(8,128)S(1)}, u32[]{:S(2)}, u32[]{:S(2)}) collective-permute-start(f32[8,7040]{1,0:T(8,128)S(1)} %blocks.1.own), channel_id=1, source_target_pairs={{0,1},{1,0},{2,3},{3,2},{4,5},{5,4},{6,7},{7,6},{8,9},{9,8},{10,11... | collective-permute-start | bytes 675848 | tf_op jit(solution)/shard_map/ppermute | solution.py:409
  8.7 9.9 %collective-permute-start.1 = (f32[8,7040]{1,0:T(8,128)S(1)}, f32[8,7040]{1,0:T(8,128)S(1)}, u32[]{:S(2)}, u32[]{:S(2)}) collective-permute-start(f32[8,7040]{1,0:T(8,128)S(1)} %blocks.1.own), channel_id=1, source_target_pairs={{0,32},{1,2},{2,1},{3,4},{4,3},{5,6},{6,5},{7,8},{8,7},{9,10},{10,... | collective-permute-start | bytes 675848 | tf_op jit(solution)/shard_map/ppermute | solution.py:410
  18.5 8.0 %collective-permute-start.2 = (f32[7,16,128]{2,1,0:T(8,128)S(1)}, f32[7,16,128]{2,1,0:T(8,128)S(1)}, u32[]{:S(2)}, u32[]{:S(2)}) collective-permute-start(f32[7,16,128]{2,1,0:T(8,128)S(1)} %edge.1), channel_id=1, source_target_pairs={{0,1},{1,0},{2,3},{3,2},{4,5},{5,4},{6,7},{7,6},{8,9},{9,8},{10,11... | collective-permute-start | bytes 172040 | tf_op jit(solution)/shard_map/ppermute | solution.py:418
  18.6 7.9 %collective-permute-start.3 = (f32[7,16,128]{2,1,0:T(8,128)S(1)}, f32[7,16,128]{2,1,0:T(8,128)S(1)}, u32[]{:S(2)}, u32[]{:S(2)}) collective-permute-start(f32[7,16,128]{2,1,0:T(8,128)S(1)} %get-tuple-element.8), channel_id=1, source_target_pairs={{0,32},{1,2},{2,1},{3,4},{4,3},{5,6},{6,5},{7,8},{8,7},{9,10},{10,... | collective-permute-start | bytes 172040 | tf_op jit(solution)/shard_map/ppermute | solution.py:416

commit v6 on v5

--- a/solution.py
+++ b/solution.py
@@ -189,6 +189,7 @@
     even_slab = lax.rem(lax.axis_index("dom"), 2) == 0
     send_chip[0:2] = jnp.where(even_slab, own[0:2], own[CX - 2 : CX])
     put_tail(other, send_chip)
+    send_chip[2 + TAIL // 256 :] = own[0:4]
 
 
 def edge_kernel(own, other, send_core):
@@ -410,7 +411,7 @@
     dots_chip = lax.ppermute(packed, ("band", "dom"), chip_pairs)
 
     rim = (2 + TAIL // 256, WY, CZ)
-    own, send_chip = call(own_kernel, "own_window", ((CX, WY, CZ), rim), [VMEM] * 2)(
+    own, send_chip = call(own_kernel, "own_window", ((CX, WY, CZ), (rim[0] + 4, WY, CZ)), [VMEM] * 2)(
         windows, dots_core
     )
     chip = lax.ppermute(send_chip, ("band", "dom"), chip_pairs)

time: 43.3 us -> 39.2 us (0.905)
  starting transfers between devices: 16.9 us -> 15.2 us
  waiting for transfers between devices: 3.64 us -> 2.52 us
  Pallas kernels: 6.39 us -> 5.57 us
  blocking collectives: 13.8 us -> 13.3 us
    ppermute x1, waiting for transfers between devices: 3.19 us -> 0.01 us  [body(): dots_chip = lax.ppermute(packed, ('band', 'dom'), chip_pairs)]
    ppermute x1, waiting for transfers between devices: 0.01 us -> 2.07 us  [body(): chip = lax.ppermute(send_chip, ('band', 'dom'), chip_pairs)]
    ppermute x1, starting transfers between devices: 5.44 us -> 3.68 us  [body(): chip = lax.ppermute(send_chip, ('band', 'dom'), chip_pairs)]
    pallas_call x1, Pallas kernels: 2.43 us -> 1.77 us  [body(): call(place_kernel, 'place_spheres', (FX + 6, 2, 2, WY, CZ), [VMEM] * 3, [...]
    all_to_all x1, blocking collectives: 13.8 us -> 13.3 us  [body(): gathered = lax.all_to_all(result, 'band', 0, 0)]
  transfers between devices with their start and end apart: 5 -> 5, of which waited for: 2 -> 2; matrix products, arithmetic and copies ran while one was open for 0% -> 0% of each run, Pallas kernels for 7% -> 6%
where the time goes in v6:
time: 39.2 us; the launch traced here: 39 us
  starting transfers between devices  15.2 us (39%)
  blocking collectives  13.3 us (34%)
  Pallas kernels  5.57 us (14%)
  waiting for transfers between devices  2.52 us (6%)
  local copies, waits for them, and re-layouts  1.64 us (4%)
  between operations  0.74 us (2%)
    all_to_all x1, blocking collectives, body(): gathered = lax.all_to_all(result, 'band', 0, 0)  13.3 us
    ppermute x1, starting transfers between devices, body(): dots_chip = lax.ppermute(packed, ('band', 'dom'), chip_pairs)  6.19 us
    all_to_all x1, starting transfers between devices, body(): windows = lax.all_to_all(windows, 'band', 0, 0)  5.1 us
    ppermute x1, starting transfers between devices, body(): chip = lax.ppermute(send_chip, ('band', 'dom'), chip_pairs)  3.68 us
    ppermute x1, waiting for transfers between devices, body(): chip = lax.ppermute(send_chip, ('band', 'dom'), chip_pairs)  2.07 us
    pallas_call x1, Pallas kernels, body(): call(main_kernel, 'potential_of', (PARTS, CX * YB, CZ), [VMEM] * 4, [pltp...  1.88 us
    pallas_call x1, Pallas kernels, body(): call(place_kernel, 'place_spheres', (FX + 6, 2, 2, WY, CZ), [VMEM] * 3, [...  1.77 us
    unnamed x8, local copies, waits for them, and re-layouts  1.64 us
  transfers between devices with their start and end apart: 5, of which 2 were waited for; matrix products, arithmetic and copies ran while one was open for 0% of the time, Pallas kernels for 6%

profile of v6, /device:TPU:4, one launch (start us, length us, event | category | flops | bytes accessed | tf_op | source)
XLA Modules:
  0.0 39.0 jit_solution(12145302217955493792)
XLA Ops:
  0.0 0.0 copy-start.1
  0.0 1.0 %copy-done.1 = f32[1,6,96,128]{3,2,1,0:T(8,128)S(1)} copy-done((f32[1,6,96,128]{3,2,1,0:T(8,128)S(1)}, f32[1,6,96,128]{3,2,1,0:T(8,128)}, u32[]{:S(2)}) %copy-start.1) | copy-done | bytes 294936
  1.0 0.0 copy-start
  1.0 0.8 %windows.1 = f32[8,6,16,128]{3,2,1,0:T(8,128)} custom-call(f32[1,6,96,128]{3,2,1,0:T(8,128)S(1)} %copy-done.1), custom_call_target="tpu_custom_call" | custom-call | tf_op jit(solution)/shard_map/windows/pallas_call | solution.py:401
  1.7 5.1 %all-to-all-start = ((f32[8,6,16,128]{3,2,1,0:T(8,128)}), f32[8,6,16,128]{3,2,1,0:T(8,128)S(1)}, u32[]{:S(2)}, u32[]{:S(2)}) async-start(f32[8,6,16,128]{3,2,1,0:T(8,128)} %windows.1), calls=%async_computation | async-start | bytes 786432 | tf_op jit(solution)/shard_map/all_to_all | solution.py:402
  7.5 0.0 copy-start.3
  7.5 0.0 copy-start.2
  7.5 0.0 copy-done
  7.5 0.7 %copy-done.3 = bf16[9,8]{0,1:T(8,128)(2,1)S(1)} copy-done((bf16[9,8]{0,1:T(8,128)(2,1)S(1)}, bf16[9,8]{0,1:T(8,128)(2,1)}, u32[]{:S(2)}) %copy-start.3) | copy-done | bytes 168
  8.2 0.0 copy-done.2
  8.2 0.4 blocks.1.own
  8.6 0.1 collective-permute-start
  8.7 6.2 %collective-permute-start.1 = (f32[8,7040]{1,0:T(8,128)S(1)}, f32[8,7040]{1,0:T(8,128)S(1)}, u32[]{:S(2)}, u32[]{:S(2)}) collective-permute-start(f32[8,7040]{1,0:T(8,128)S(1)} %blocks.1.own), channel_id=1, source_target_pairs={{0,32},{1,2},{2,1},{3,4},{4,3},{5,6},{6,5},{7,8},{8,7},{9,10},{10,... | collective-permute-start | bytes 675848 | tf_op jit(solution)/shard_map/ppermute | solution.py:411
  14.9 0.0 collective-permute-done.other.core
  14.9 0.4 %all-to-all-done.windows = f32[8,6,16,128]{3,2,1,0:T(8,128)S(1)} async-done(((f32[8,6,16,128]{3,2,1,0:T(8,128)}), f32[8,6,16,128]{3,2,1,0:T(8,128)S(1)}, u32[]{:S(2)}, u32[]{:S(2)}) %all-to-all-start) | async-done | bytes 393248 | tf_op jit(solution)/shard_map/all_to_all | solution.py:402
  15.3 3.7 %collective-permute-start.3 = (f32[11,16,128]{2,1,0:T(8,128)S(1)}, f32[11,16,128]{2,1,0:T(8,128)S(1)}, u32[]{:S(2)}, u32[]{:S(2)}) collective-permute-start(f32[11,16,128]{2,1,0:T(8,128)S(1)} %get-tuple-element.8), channel_id=1, source_target_pairs={{0,32},{1,2},{2,1},{3,4},{4,3},{5,6},{6,5},{7,8},{8,7},{9,10},{10,... | collective-permute-start | bytes 270344 | tf_op jit(solution)/shard_map/ppermute | solution.py:417
  19.0 0.0 collective-permute-done.1.other.chip
  19.0 0.1 collective-permute-start.2
  19.1 1.8 %place_spheres.1.dots = f32[18,2,2,16,128]{4,3,2,1,0:T(8,128)S(1)} custom-call(f32[8,7040]{1,0:T(8,128)S(1)} %blocks.1.own, f32[8,7040]{1,0:T(8,128)S(1)} %collective-permute-done.other.core, f32[8,7040]{1,0:T(8,128)S(1)} %collective-permute-done.1.other.chip), custom_call_target="tpu_custom_call" | custom-call | tf_op jit(solution)/shard_map/place_spheres/pallas_call | solution.py:420
  20.9 0.0 collective-permute-done.2.core
  20.9 2.1 %collective-permute-done.3.chip = f32[11,16,128]{2,1,0:T(8,128)S(1)} collective-permute-done((f32[11,16,128]{2,1,0:T(8,128)S(1)}, f32[11,16,128]{2,1,0:T(8,128)S(1)}, u32[]{:S(2)}, u32[]{:S(2)}) %collective-permute-start.3) | collective-permute-done | bytes 90144 | tf_op jit(solution)/shard_map/ppermute | solution.py:417
  23.0 1.9 %potential_of.1 = f32[8,72,128]{2,1,0:T(8,128)S(1)} custom-call(f32[6,16,128]{2,1,0:T(8,128)S(1)} %get-tuple-element.7.own, f32[7,16,128]{2,1,0:T(8,128)S(1)} %collective-permute-done.2.core, f32[11,16,128]{2,1,0:T(8,128)S(1)} %collective-permute-done.3.chip, f32[18,2,2,16,128]{4,3,2,1,0:T(8,128)S(1)} %place_spheres.1.dots), custom_call_target="tpu_custom_call" | custom-call | tf_op jit(solution)/shard_map/potential_of/pallas_call | solution.py:434
  24.9 13.3 %all_to_all.10.pieces = f32[8,72,128]{2,1,0:T(8,128)S(1)} all-to-all(f32[8,72,128]{2,1,0:T(8,128)S(1)} %potential_of.1), channel_id=1, replica_groups=mesh['band'=8,'dom'=32] {'band'}, dimensions={0} | all-to-all | bytes 589824 | tf_op jit(solution)/shard_map/all_to_all | solution.py:451
  38.2 0.7 %join.1 = f32[6,96,128]{2,1,0:T(8,128)} custom-call(f32[8,72,128]{2,1,0:T(8,128)S(1)} %all_to_all.10.pieces), custom_call_target="tpu_custom_call" | custom-call | tf_op jit(solution)/shard_map/join/pallas_call | solution.py:452
  (2 shorter events, 0.0 us)
Async XLA Ops:
  0.0 1.0 %copy-start.1 = (f32[1,6,96,128]{3,2,1,0:T(8,128)S(1)}, f32[1,6,96,128]{3,2,1,0:T(8,128)}, u32[]{:S(2)}) copy-start(f32[1,6,96,128]{3,2,1,0:T(8,128)} %cells.1) | copy-start | bytes 884740
  1.0 6.6 %copy-start = (bf16[8,9,6912]{2,0,1:T(8,128)(2,1)S(1)}, bf16[8,9,6912]{2,0,1:T(8,128)(2,1)}, u32[]{:S(2)}) copy-start(bf16[8,9,6912]{2,0,1:T(8,128)(2,1)} %param.7) | copy-start | bytes 2985988
  1.7 13.6 %all-to-all-start = ((f32[8,6,16,128]{3,2,1,0:T(8,128)}), f32[8,6,16,128]{3,2,1,0:T(8,128)S(1)}, u32[]{:S(2)}, u32[]{:S(2)}) async-start(f32[8,6,16,128]{3,2,1,0:T(8,128)} %windows.1), calls=%async_computation | async-start | bytes 786432 | tf_op jit(solution)/shard_map/all_to_all | solution.py:402
  7.5 0.7 %copy-start.3 = (bf16[9,8]{0,1:T(8,128)(2,1)S(1)}, bf16[9,8]{0,1:T(8,128)(2,1)}, u32[]{:S(2)}) copy-start(bf16[9,8]{0,1:T(8,128)(2,1)} %param.6) | copy-start | bytes 436
  7.5 0.7 %copy-start.2 = (s32[3,8]{1,0:T(4,128)S(1)}, s32[3,8]{1,0:T(4,128)}, u32[]{:S(2)}) copy-start(s32[3,8]{1,0:T(4,128)} %offsets.1) | copy-start | bytes 292
  8.6 6.3 %collective-permute-start = (f32[8,7040]{1,0:T(8,128)S(1)}, f32[8,7040]{1,0:T(8,128)S(1)}, u32[]{:S(2)}, u32[]{:S(2)}) collective-permute-start(f32[8,7040]{1,0:T(8,128)S(1)} %blocks.1.own), channel_id=1, source_target_pairs={{0,1},{1,0},{2,3},{3,2},{4,5},{5,4},{6,7},{7,6},{8,9},{9,8},{10,11... | collective-permute-start | bytes 675848 | tf_op jit(solution)/shard_map/ppermute | solution.py:410
  8.7 10.3 %collective-permute-start.1 = (f32[8,7040]{1,0:T(8,128)S(1)}, f32[8,7040]{1,0:T(8,128)S(1)}, u32[]{:S(2)}, u32[]{:S(2)}) collective-permute-start(f32[8,7040]{1,0:T(8,128)S(1)} %blocks.1.own), channel_id=1, source_target_pairs={{0,32},{1,2},{2,1},{3,4},{4,3},{5,6},{6,5},{7,8},{8,7},{9,10},{10,... | collective-permute-start | bytes 675848 | tf_op jit(solution)/shard_map/ppermute | solution.py:411
  15.3 7.7 %collective-permute-start.3 = (f32[11,16,128]{2,1,0:T(8,128)S(1)}, f32[11,16,128]{2,1,0:T(8,128)S(1)}, u32[]{:S(2)}, u32[]{:S(2)}) collective-permute-start(f32[11,16,128]{2,1,0:T(8,128)S(1)} %get-tuple-element.8), channel_id=1, source_target_pairs={{0,32},{1,2},{2,1},{3,4},{4,3},{5,6},{6,5},{7,8},{8,7},{9,10},{10,... | collective-permute-start | bytes 270344 | tf_op jit(solution)/shard_map/ppermute | solution.py:417
  19.0 1.9 %collective-permute-start.2 = (f32[7,16,128]{2,1,0:T(8,128)S(1)}, f32[7,16,128]{2,1,0:T(8,128)S(1)}, u32[]{:S(2)}, u32[]{:S(2)}) collective-permute-start(f32[7,16,128]{2,1,0:T(8,128)S(1)} %edge.1), channel_id=1, source_target_pairs={{0,1},{1,0},{2,3},{3,2},{4,5},{5,4},{6,7},{7,6},{8,9},{9,8},{10,11... | collective-permute-start | bytes 172040 | tf_op jit(solution)/shard_map/ppermute | solution.py:419
